TPU v7x, 32 devices: a whole 2x2x4 slice. The times are simulated.
32 devices in a mesh: groups: 2 (over y), expert: 16 (over z, x, core).
Axes of the slice: x: 2, y: 2, z: 4, core: 2. Of those that a mesh axis runs over, the one named last changes fastest.
Arguments:
- tokens: bfloat16 [2048, 2048], P(('groups', 'expert')), parts along dimension 0, may hold values from -6 to 6
- scales: bfloat16 [2048, 16], P(('groups', 'expert')), parts along dimension 0, may hold values from 0.29882812 to 3
- expert_ids: int32 [2048, 8], P(('groups', 'expert')), parts along dimension 0, may hold values from 0 to 15, all different within a row; in each aligned block of 64 rows (0 to 63, 64 to 127, ...) at most 64 rows name the same one
- gate_weights: float32 [2048, 8], P(('groups', 'expert')), parts along dimension 0, may hold values from 0.02 to 0.3
- w_gate: bfloat16 [16, 2048, 768], P('expert'), may hold values from -0.125 to 0.125
- w_up: bfloat16 [16, 2048, 768], P('expert'), may hold values from -0.125 to 0.125
- w_down: bfloat16 [16, 768, 2048], P('expert'), may hold values from -0.21875 to 0.21875
Outputs:
- combined: bfloat16 [2048, 2048], P(('groups', 'expert')), parts along dimension 0
There are 2 independent parts, one for each index of `groups`. A program takes and returns all parts, laid end to end along the dimension named above; an argument that names none is the same for every part. Nothing has to cross between parts.
Inputs may be any that keep to these rules, and one draw needn't show every extreme that they name: `expert_ids`: each token names 8 different experts. Among the 64 tokens of one index of expert (aligned blocks of rows) no expert is named by more than 64 tokens, and in some blocks some expert is named by exactly 64.
All inputs are finite; a program needn't handle non-finite values.
Results may differ from a plain program's by a relative error of at most 0.0071.
Values may be sent and summed in bfloat16 or wider, within the bound.
No kernel may reach another device: no remote copies, remote signals or barrier semaphores. Data moves between devices by JAX's collectives and lax.ppermute only.
A program may use at most 128 MiB of HBM per device.

v0:
```python
import jax
import jax.numpy as jnp
from jax import lax
from jax.sharding import PartitionSpec as P


def dequantize(values, scales):
    array_shape = values.shape
    blocks = scales.shape[-1]
    split_shape = array_shape[:-1] + (blocks, array_shape[-1] // blocks)
    scaled = values.astype(jnp.float32).reshape(split_shape) * scales.astype(jnp.float32)[..., None]
    return scaled.reshape(array_shape).astype(jnp.bfloat16)


def apply_experts(values, scale_rows, w_gate, w_up, w_down):
    inputs = dequantize(values, scale_rows)
    gate_part = jnp.einsum("pecd,edf->pecf", inputs, w_gate, preferred_element_type=jnp.float32)
    up_part = jnp.einsum("pecd,edf->pecf", inputs, w_up, preferred_element_type=jnp.float32)
    hidden = (jax.nn.silu(gate_part) * up_part).astype(jnp.bfloat16)
    return jnp.einsum("pecf,efd->pecd", hidden, w_down, preferred_element_type=jnp.float32).astype(
        jnp.bfloat16
    )


def on_device(tokens, scales, expert_ids, gate_weights, w_gate, w_up, w_down):
    peer_count = lax.axis_size("expert")
    token_count, feature_width = tokens.shape
    top_count = expert_ids.shape[1]
    local_experts = w_gate.shape[0]
    expert_total = peer_count * local_experts
    capacity = 2 * token_count * top_count // expert_total
    blocks = scales.shape[1]
    flat_ids = expert_ids.reshape(-1)
    onehot = (flat_ids[:, None] == jnp.arange(expert_total, dtype=jnp.int32)[None, :]).astype(
        jnp.int32
    )
    position = jnp.sum((jnp.cumsum(onehot, axis=0) - onehot) * onehot, axis=1)
    slot_index = flat_ids * capacity + position
    source_token = jnp.arange(token_count * top_count, dtype=jnp.int32) // top_count
    send_values = (
        jnp.zeros((expert_total * capacity, feature_width), jnp.bfloat16)
        .at[slot_index]
        .set(tokens[source_token])
    )
    send_values = send_values.reshape(peer_count, local_experts, capacity, feature_width)
    send_scales = (
        jnp.zeros((expert_total * capacity, blocks), jnp.bfloat16)
        .at[slot_index]
        .set(scales[source_token])
    )
    send_scales = send_scales.reshape(peer_count, local_experts, capacity, blocks)
    outputs = apply_experts(
        lax.all_to_all(send_values, "expert", split_axis=0, concat_axis=0, tiled=True),
        lax.all_to_all(send_scales, "expert", split_axis=0, concat_axis=0, tiled=True),
        w_gate,
        w_up,
        w_down,
    )
    returned = lax.all_to_all(outputs, "expert", split_axis=0, concat_axis=0, tiled=True)
    gathered = returned.reshape(expert_total * capacity, feature_width)[slot_index]
    gathered = gathered.reshape(token_count, top_count, feature_width)
    combined = jnp.sum(gate_weights[:, :, None] * gathered.astype(jnp.float32), axis=1)
    return combined.astype(jnp.bfloat16)


def solution(mesh):
    return jax.shard_map(
        on_device,
        mesh=mesh,
        in_specs=(
            P(("groups", "expert"), None),
            P(("groups", "expert"), None),
            P(("groups", "expert"), None),
            P(("groups", "expert"), None),
            P("expert", None, None),
            P("expert", None, None),
            P("expert", None, None),
        ),
        out_specs=P(("groups", "expert"), None),
        check_vma=False,
    )
```

profile of v0, /device:TPU:12, one launch (start us, length us, event | category | flops | bytes accessed | tf_op | source)
XLA Modules:
  0.0 258.4 jit_solution(4109401206095571712)
XLA Ops:
  0.0 0.0 copy-start
  0.0 0.9 copy.35
  0.9 0.1 eq.29
  1.0 0.1 eq.25
  1.1 0.7 broadcast_multiply_fusion
  1.8 1.2 reduce-window.6
  3.0 0.2 slice_reduce_fusion
  3.2 0.1 copy.34
  3.3 0.1 mul.51
  3.4 0.8 copy.38
  4.2 0.1 fusion.26
  4.3 3.1 %scatter_custom_fusion.1 = bf16[1024,16]{1,0:T(8,128)(2,1)S(1)} fusion(s32[512]{0:T(512)S(1)} %bitcast.106, bf16[64,16]{1,0:T(8,128)(2,1)S(1)} %copy.38, s32[1024]{0:T(1024)S(1)} %pad_clamp_fusion.1, bf16[]{:T(256)} %constant.26.clone.1), kind=kCustom, calls=%fused_computation.26 | custom fusion | bytes 32770 | tf_op jit(solution)/shard_map/scatter | solution.py:49
  7.4 0.1 copy.40
  7.5 0.7 reshape.203
  8.3 6.3 %all-to-all-start.1 = ((bf16[16,2,512]{2,1,0:T(2,128)(2,1)}), bf16[16,2,512]{2,1,0:T(2,128)(2,1)S(1)}, u32[]{:S(2)}, u32[]{:S(2)}) async-start(bf16[16,2,512]{2,1,0:T(2,128)(2,1)} %reshape.203), calls=%async_computation.1 | async-start | bytes 65536 | tf_op jit(solution)/shard_map/all_to_all | solution.py:54
  14.5 13.2 %scatter_custom_fusion = bf16[1024,2048]{1,0:T(8,128)(2,1)} fusion(s32[512]{0:T(512)S(1)} %bitcast.107, bf16[64,2048]{1,0:T(8,128)(2,1)} %param.7, s32[1024]{0:T(1024)S(1)} %pad_clamp_fusion.1, bf16[]{:T(256)} %constant.26.clone.1), kind=kCustom, calls=%fused_computation.22 | custom fusion | bytes 4194816 | tf_op jit(solution)/shard_map/scatter | solution.py:43
  27.7 0.0 all-to-all-done.1
  27.7 6.0 %all-to-all-start = ((bf16[16,1,64,2048]{3,2,1,0:T(8,128)(2,1)}), bf16[16,1,64,2048]{3,2,1,0:T(8,128)(2,1)}, u32[]{:S(2)}, u32[]{:S(2)}) async-start(bf16[16,1,64,2048]{3,2,1,0:T(8,128)(2,1)} %bitcast.103), calls=%async_computation | async-start | bytes 8388608 | tf_op jit(solution)/shard_map/all_to_all | solution.py:53
  33.7 0.1 reshape.204
  33.9 1.0 copy.41
  34.9 5.8 %mul.55 = f32[16,64,16,128]{3,2,1,0:T(8,128)} broadcast(f32[16,64,16]{2,1,0:T(8,128)} %copy.41), dimensions={0,1,2} | broadcast | bytes 8454144 | tf_op jit(solution)/shard_map/mul | solution.py:11
  40.7 9.3 %mul.56 = f32[16,1,64,2048]{3,2,1,0:T(8,128)} reshape(f32[16,64,16,128]{3,2,1,0:T(8,128)} %mul.55) | data formatting | bytes 16777216 | tf_op jit(solution)/shard_map/mul | solution.py:11
  50.0 74.6 %all-to-all-done = bf16[16,1,64,2048]{3,2,1,0:T(8,128)(2,1)} async-done(((bf16[16,1,64,2048]{3,2,1,0:T(8,128)(2,1)}), bf16[16,1,64,2048]{3,2,1,0:T(8,128)(2,1)}, u32[]{:S(2)}, u32[]{:S(2)}) %all-to-all-start) | async-done | bytes 4194336 | tf_op jit(solution)/shard_map/all_to_all | solution.py:53
  124.5 10.6 %fusion.4 = f32[16,64,768]{2,1,0:T(8,128)} fusion(bf16[1,2048,768]{2,1,0:T(8,128)(2,1)} %param.12, f32[16,1,64,2048]{3,2,1,0:T(8,128)} %mul.56, bf16[16,1,64,2048]{3,2,1,0:T(8,128)(2,1)} %all-to-all-done), kind=kOutput, calls=%fused_computation.13 | convolution fusion | flops 3227516928 | bytes 18874368 | tf_op jit(solution)/shard_map/pecd,edf->pecf/dot_general | solution.py:18
  135.2 0.0 copy-done
  135.2 13.5 %convert_bitcast_fusion = bf16[16,1,64,2048]{3,2,1,0:T(8,128)(2,1)} fusion(bf16[1,768,2048]{2,1,0:T(8,128)(2,1)S(1)} %copy-done, f32[16,64,768]{2,1,0:T(8,128)} %fusion.4, bf16[1,2048,768]{2,1,0:T(8,128)(2,1)} %param.11, f32[16,1,64,2048]{3,2,1,0:T(8,128)} %mul.56, bf16[16,1,64,2048]{3,2,1,0:T(8,128)(2,1)} %all-to-all-done), kind=kOutput, calls=%fused_computation.9 | convolution fusion | flops 6455558144 | bytes 26214400 | tf_op jit(solution)/shard_map/pecf,efd->pecd/dot_general | solution.py:20
  148.7 6.7 %all-to-all-start.2 = ((bf16[16,1,64,2048]{3,2,1,0:T(8,128)(2,1)}), bf16[16,1,64,2048]{3,2,1,0:T(8,128)(2,1)}, u32[]{:S(2)}, u32[]{:S(2)}) async-start(bf16[16,1,64,2048]{3,2,1,0:T(8,128)(2,1)} %convert_bitcast_fusion), calls=%async_computation.2 | async-start | bytes 8388608 | tf_op jit(solution)/shard_map/all_to_all | solution.py:59
  155.4 0.0 copy-done.1
  155.4 0.1 copy.33
  155.5 90.7 %all-to-all-done.2 = bf16[16,1,64,2048]{3,2,1,0:T(8,128)(2,1)} async-done(((bf16[16,1,64,2048]{3,2,1,0:T(8,128)(2,1)}), bf16[16,1,64,2048]{3,2,1,0:T(8,128)(2,1)}, u32[]{:S(2)}, u32[]{:S(2)}) %all-to-all-start.2) | async-done | bytes 4194336 | tf_op jit(solution)/shard_map/all_to_all | solution.py:59
  246.2 8.0 %gather_fusion = bf16[512,2048]{1,0:T(8,128)(2,1)} fusion(bf16[1024,2048]{1,0:T(8,128)(2,1)} %bitcast.27, s32[1024]{0:T(1024)S(1)} %pad_clamp_fusion), kind=kCustom, calls=%fused_computation.2 | custom fusion | bytes 4196352 | tf_op jit(solution)/shard_map/gather | solution.py:60
  254.2 4.1 %fusion.1 = bf16[64,2048]{1,0:T(8,128)(2,1)} fusion(bf16[512,2048]{1,0:T(8,128)(2,1)} %gather_fusion, f32[64,8]{1,0:T(8,128)S(1)} %copy.33), kind=kLoop, calls=%fused_computation.8 | loop fusion | flops 3014656 | bytes 2361344 | tf_op jit(solution)/shard_map/reduce_sum | solution.py:62
  (9 shorter events, 0.1 us)
Async XLA Ops:
  0.0 135.2 %copy-start = (bf16[1,768,2048]{2,1,0:T(8,128)(2,1)S(1)}, bf16[1,768,2048]{2,1,0:T(8,128)(2,1)}, u32[]{:S(2)}) copy-start(bf16[1,768,2048]{2,1,0:T(8,128)(2,1)} %param.13) | copy-start | bytes 9437188
  8.3 19.4 %all-to-all-start.1 = ((bf16[16,2,512]{2,1,0:T(2,128)(2,1)}), bf16[16,2,512]{2,1,0:T(2,128)(2,1)S(1)}, u32[]{:S(2)}, u32[]{:S(2)}) async-start(bf16[16,2,512]{2,1,0:T(2,128)(2,1)} %reshape.203), calls=%async_computation.1 | async-start | bytes 65536 | tf_op jit(solution)/shard_map/all_to_all | solution.py:54
  27.7 96.8 %all-to-all-start = ((bf16[16,1,64,2048]{3,2,1,0:T(8,128)(2,1)}), bf16[16,1,64,2048]{3,2,1,0:T(8,128)(2,1)}, u32[]{:S(2)}, u32[]{:S(2)}) async-start(bf16[16,1,64,2048]{3,2,1,0:T(8,128)(2,1)} %bitcast.103), calls=%async_computation | async-start | bytes 8388608 | tf_op jit(solution)/shard_map/all_to_all | solution.py:53
  148.7 6.7 %copy-start.1 = (f32[64,8]{0,1:T(8,128)S(1)}, f32[64,8]{0,1:T(8,128)}, u32[]{:S(2)}) copy-start(f32[64,8]{0,1:T(8,128)} %param.10) | copy-start | bytes 6148
  148.7 97.5 %all-to-all-start.2 = ((bf16[16,1,64,2048]{3,2,1,0:T(8,128)(2,1)}), bf16[16,1,64,2048]{3,2,1,0:T(8,128)(2,1)}, u32[]{:S(2)}, u32[]{:S(2)}) async-start(bf16[16,1,64,2048]{3,2,1,0:T(8,128)(2,1)} %convert_bitcast_fusion), calls=%async_computation.2 | async-start | bytes 8388608 | tf_op jit(solution)/shard_map/all_to_all | solution.py:59
where the time goes:
time: 261 us; the launch traced here: 258 us
  waiting for transfers between devices  165 us (63%)
  local copies, waits for them, and re-layouts  43.7 us (17%)
  matrix products  24.2 us (9%)
  starting transfers between devices  19 us (7%)
  other arithmetic  6.16 us (2%)
    all_to_all x1, waiting for transfers between devices, on_device(): lax.all_to_all(outputs, 'expert', split_axis=0, concat_axis=0, tiled=True)  90.7 us
    all_to_all x1, waiting for transfers between devices, on_device(): lax.all_to_all(send_values, 'expert', split_axis=0, concat_axis=0, tiled=...  74.6 us
    mul x3, local copies, waits for them, and re-layouts, dequantize(): values.astype(jnp.float32).reshape(split_shape)  16.1 us
    dot_general x1, matrix products, apply_experts(): jnp.einsum('pecf,efd->pecd', hidden, w_down, preferred_element_type=jnp.f...  13.5 us
    scatter x1, local copies, waits for them, and re-layouts, on_device(): send_values = jnp.zeros((expert_total * capacity, feature_width), jnp.bfl...  13.2 us
    dot_general x1, matrix products, apply_experts(): jnp.einsum('pecd,edf->pecf', inputs, w_up, preferred_element_type=jnp.flo...  10.6 us
    gather x1, local copies, waits for them, and re-layouts, on_device(): returned.reshape(expert_total * capacity, feature_width)[slot_index]  8 us
    all_to_all x1, starting transfers between devices, on_device(): lax.all_to_all(outputs, 'expert', split_axis=0, concat_axis=0, tiled=True)  6.69 us
  transfers between devices with their start and end apart: 3, of which 2 were waited for; matrix products, arithmetic and copies ran while one was open for 11% of the time, Pallas kernels for 0%

commit v1 on v0

--- a/solution.py
+++ b/solution.py
@@ -1,7 +1,13 @@
+import functools
+
 import jax
 import jax.numpy as jnp
 from jax import lax
+from jax.experimental import pallas as pl
+from jax.experimental.pallas import tpu as pltpu
 from jax.sharding import PartitionSpec as P
+
+LANES = 128
 
 
 def dequantize(values, scales):
@@ -22,7 +28,7 @@
     )
 
 
-def on_device(tokens, scales, expert_ids, gate_weights, w_gate, w_up, w_down):
+def routed(tokens, scales, expert_ids, gate_weights, w_gate, w_up, w_down):
     peer_count = lax.axis_size("expert")
     token_count, feature_width = tokens.shape
     top_count = expert_ids.shape[1]
@@ -63,6 +69,122 @@
     return combined.astype(jnp.bfloat16)
 
 
+def pack_rows(tokens, scales, expert_ids, gate_weights, expert_total):
+    activations = dequantize(tokens, scales)
+    chosen = expert_ids[:, :, None] == jnp.arange(expert_total, dtype=jnp.int32)[None, None, :]
+    dense = jnp.sum(jnp.where(chosen, gate_weights[:, :, None], 0.0), axis=1)
+    terms = []
+    for _ in range(3):
+        term = dense.astype(jnp.bfloat16)
+        dense = dense - term.astype(jnp.float32)
+        terms.append(term)
+    spare = -3 * expert_total % LANES
+    terms.append(jnp.zeros((tokens.shape[0], spare), jnp.bfloat16))
+    return jnp.concatenate([activations] + terms, axis=1)
+
+
+def expert_kernel(expert_total, me_ref, a0, a1, a2, a3, gate_ref, up_ref, down_ref, q0, q1, q2, q3, rows, total):
+    step = pl.program_id(0)
+    blocks = (a0, a1, a2, a3)
+    count = a0.shape[0]
+    width = down_ref.shape[2]
+
+    @pl.when(step == 0)
+    def _():
+        for index, block in enumerate(blocks):
+            rows[index * count : (index + 1) * count, :] = block[:, :width]
+
+    inputs = rows[...]
+    gate_part = jnp.dot(inputs, gate_ref[0], preferred_element_type=jnp.float32)
+    up_part = jnp.dot(inputs, up_ref[0], preferred_element_type=jnp.float32)
+    hidden = (gate_part / (1.0 + jnp.exp(-gate_part)) * up_part).astype(jnp.bfloat16)
+    product = jnp.dot(hidden, down_ref[0], preferred_element_type=jnp.float32)
+
+    @pl.when(step == 0)
+    def _():
+        total[...] = product
+
+    @pl.when(step > 0)
+    def _():
+        total[...] += product
+
+    @pl.when(step == pl.num_programs(0) - 1)
+    def _():
+        for index, (block, out) in enumerate(zip(blocks, (q0, q1, q2, q3), strict=True)):
+            terms = block[:, width:].astype(jnp.float32)
+            lane = lax.broadcasted_iota(jnp.int32, terms.shape, 1) % expert_total
+            weight = jnp.sum(jnp.where(lane == me_ref[0], terms, 0.0), axis=1, keepdims=True)
+            result = total[index * count : (index + 1) * count, :].astype(jnp.bfloat16)
+            out[...] = (weight * result.astype(jnp.float32)).astype(out.dtype)
+
+
+def weighted_outputs(expert_total, me, blocks, w_gate, w_up, w_down):
+    count, packed = blocks[0].shape
+    hidden_width, width = w_down.shape[1:]
+    chunk = 256
+    whole = pl.BlockSpec((count, packed), lambda s: (0, 0))
+    out = pl.BlockSpec((count, width), lambda s: (0, 0))
+    rows = 4 * count
+    return pl.pallas_call(
+        functools.partial(expert_kernel, expert_total),
+        grid=(hidden_width // chunk,),
+        in_specs=[pl.BlockSpec(memory_space=pltpu.SMEM)]
+        + [whole] * 4
+        + [pl.BlockSpec((1, width, chunk), lambda s: (0, 0, s))] * 2
+        + [pl.BlockSpec((1, chunk, width), lambda s: (0, s, 0))],
+        out_specs=[out] * 4,
+        out_shape=[
+            jax.ShapeDtypeStruct((count, width), jnp.bfloat16 if index % 2 else jnp.float32)
+            for index in range(4)
+        ],
+        scratch_shapes=[pltpu.VMEM((rows, width), jnp.bfloat16), pltpu.VMEM((rows, width), jnp.float32)],
+        compiler_params=pltpu.CompilerParams(vmem_limit_bytes=32 * 2**20),
+        cost_estimate=pl.CostEstimate(
+            flops=6 * rows * width * hidden_width,
+            bytes_accessed=6 * width * hidden_width + 10 * rows * width,
+            transcendentals=rows * hidden_width,
+        ),
+    )(me, *blocks, w_gate, w_up, w_down)
+
+
+def gathered(tokens, scales, expert_ids, gate_weights, w_gate, w_up, w_down):
+    peer_count = lax.axis_size("expert")
+
+    def exchange(array, mask):
+        return lax.ppermute(array, "expert", [(i, i ^ mask) for i in range(peer_count)])
+
+    me = lax.axis_index("expert").astype(jnp.int32).reshape(1)
+    columns = range(0, peer_count, 4)
+    rows = {0: pack_rows(tokens, scales, expert_ids, gate_weights, peer_count)}
+    for z in columns[1:]:
+        rows[z] = exchange(rows[0], z)
+    for z in columns:
+        rows[z + 2] = exchange(rows[z], 2)
+    for z in columns:
+        for x in (z, z + 2):
+            rows[x + 1] = exchange(rows[x], 1)
+    sums = {}
+    for z in columns:
+        parts = weighted_outputs(peer_count, me, [rows[z + j] for j in range(4)], w_gate, w_up, w_down)
+        own = parts[0] + exchange(parts[1], 1).astype(jnp.float32)
+        other = parts[2] + exchange(parts[3], 1).astype(jnp.float32)
+        sums[z] = own + exchange(other.astype(jnp.bfloat16), 2).astype(jnp.float32)
+    combined = sums[0]
+    for z in columns[1:]:
+        combined = combined + exchange(sums[z].astype(jnp.bfloat16), z).astype(jnp.float32)
+    return combined.astype(jnp.bfloat16)
+
+
+def on_device(tokens, scales, expert_ids, gate_weights, w_gate, w_up, w_down):
+    peer_count = lax.axis_size("expert")
+    local_experts = w_gate.shape[0]
+    capacity = 2 * tokens.shape[0] * expert_ids.shape[1] // (peer_count * local_experts)
+    power_of_two = peer_count & (peer_count - 1) == 0
+    whole = capacity >= tokens.shape[0] and local_experts == 1 and peer_count >= 4 and power_of_two
+    layer = gathered if whole else routed
+    return layer(tokens, scales, expert_ids, gate_weights, w_gate, w_up, w_down)
+
+
 def solution(mesh):
     return jax.shard_map(
         on_device,

time: 261 us -> 112 us (0.43)
  the two profiles are of different devices: /device:TPU:12 before, /device:TPU:0 now
where the time goes in v1:
time: 112 us
  waiting for transfers between devices  62 us (55%)
  starting transfers between devices  21.4 us (19%)
  Pallas kernels  18.3 us (16%)
  local copies, waits for them, and re-layouts  6.93 us (6%)
  other arithmetic  3.22 us (3%)
    ppermute x30, waiting for transfers between devices, exchange(): lax.ppermute(array, 'expert', [(i, i ^ mask) for i in range(peer_count)])  62 us
    ppermute x30, starting transfers between devices, exchange(): lax.ppermute(array, 'expert', [(i, i ^ mask) for i in range(peer_count)])  21.4 us
    pallas_call x4, Pallas kernels, weighted_outputs(): pl.pallas_call(functools.partial(expert_kernel, expert_total), grid=(hidd...  18.3 us
    unnamed x8, local copies, waits for them, and re-layouts  5.67 us
  transfers between devices with their start and end apart: 30, of which 10 were waited for; matrix products, arithmetic and copies ran while one was open for 0% of the time, Pallas kernels for 16%

profile of v1, /device:TPU:0, one launch (start us, length us, event | category | flops | bytes accessed | tf_op | source)
XLA Modules:
  0.0 112.1 jit_solution(2333097653223125854)
XLA Ops:
  0.0 0.7 select_reduce_fusion
  0.8 0.8 copy.14
  1.9 1.1 %fusion = bf16[64,2048]{1,0:T(8,128)(2,1)S(1)} fusion(f32[8,8,16,128]{3,2,1,0:T(8,128)S(1)} %bitcast.6, bf16[64,2048]{1,0:T(8,128)(2,1)} %param.7), kind=kLoop, calls=%fused_computation.1 | loop fusion | flops 393216 | bytes 1048576 | tf_op jit(solution)/shard_map/convert_element_type | solution.py:18
  3.2 3.0 %collective-permute-start.1 = (bf16[64,2176]{1,0:T(8,128)(2,1)S(1)}, bf16[64,2176]{1,0:T(8,128)(2,1)S(1)}, u32[]{:S(2)}, u32[]{:S(2)}) collective-permute-start(bf16[64,2176]{1,0:T(8,128)(2,1)S(1)} %concatenate.3.a0), channel_id=1, source_target_pairs={{0,2},{1,3},{2,0},{3,1},{4,6},{5,7},{6,4},{7,5},{8,10},{9,11},{10,... | collective-permute-start | bytes 835592 | tf_op jit(solution)/shard_map/ppermute | solution.py:154
  6.2 3.6 %collective-permute-start.22 = (bf16[64,2176]{1,0:T(8,128)(2,1)S(1)}, bf16[64,2176]{1,0:T(8,128)(2,1)S(1)}, u32[]{:S(2)}, u32[]{:S(2)}) collective-permute-start(bf16[64,2176]{1,0:T(8,128)(2,1)S(1)} %concatenate.3.a0), channel_id=1, source_target_pairs={{0,12},{1,13},{2,14},{3,15},{4,8},{5,9},{6,10},{7,11},{8,4},{9,5},... | collective-permute-start | bytes 835592 | tf_op jit(solution)/shard_map/ppermute | solution.py:154
  9.8 3.0 %collective-permute-done.1.a2 = bf16[64,2176]{1,0:T(8,128)(2,1)S(1)} collective-permute-done((bf16[64,2176]{1,0:T(8,128)(2,1)S(1)}, bf16[64,2176]{1,0:T(8,128)(2,1)S(1)}, u32[]{:S(2)}, u32[]{:S(2)}) %collective-permute-start.1) | collective-permute-done | bytes 278560 | tf_op jit(solution)/shard_map/ppermute | solution.py:154
  12.8 1.8 %collective-permute-start.6 = (bf16[64,2176]{1,0:T(8,128)(2,1)S(1)}, bf16[64,2176]{1,0:T(8,128)(2,1)S(1)}, u32[]{:S(2)}, u32[]{:S(2)}) collective-permute-start(bf16[64,2176]{1,0:T(8,128)(2,1)S(1)} %concatenate.3.a0), channel_id=1, source_target_pairs={{0,4},{1,5},{2,6},{3,7},{4,0},{5,1},{6,2},{7,3},{8,12},{9,13},{10,... | collective-permute-start | bytes 835592 | tf_op jit(solution)/shard_map/ppermute | solution.py:154
  14.7 2.9 %collective-permute-done.22.a0 = bf16[64,2176]{1,0:T(8,128)(2,1)S(1)} collective-permute-done((bf16[64,2176]{1,0:T(8,128)(2,1)S(1)}, bf16[64,2176]{1,0:T(8,128)(2,1)S(1)}, u32[]{:S(2)}, u32[]{:S(2)}) %collective-permute-start.22) | collective-permute-done | bytes 278560 | tf_op jit(solution)/shard_map/ppermute | solution.py:154
  17.9 15.3 %collective-permute-done.14.a0 = bf16[64,2176]{1,0:T(8,128)(2,1)S(1)} collective-permute-done((bf16[64,2176]{1,0:T(8,128)(2,1)S(1)}, bf16[64,2176]{1,0:T(8,128)(2,1)S(1)}, u32[]{:S(2)}, u32[]{:S(2)}) %collective-permute-start.14) | collective-permute-done | bytes 278560 | tf_op jit(solution)/shard_map/ppermute | solution.py:154
  33.2 0.5 collective-permute-start.16
  33.8 1.9 %copy-done = bf16[1,2048,768]{2,1,0:T(8,128)(2,1)S(1)} copy-done((bf16[1,2048,768]{2,1,0:T(8,128)(2,1)S(1)}, bf16[1,2048,768]{2,1,0:T(8,128)(2,1)}, u32[]{:S(2)}) %copy-start) | copy-done | bytes 3145752
  35.7 1.9 %copy-done.2 = bf16[1,2048,768]{2,1,0:T(8,128)(2,1)S(1)} copy-done((bf16[1,2048,768]{2,1,0:T(8,128)(2,1)S(1)}, bf16[1,2048,768]{2,1,0:T(8,128)(2,1)}, u32[]{:S(2)}) %copy-start.2) | copy-done | bytes 3145752
  37.5 1.9 %copy-done.3 = bf16[1,768,2048]{2,1,0:T(8,128)(2,1)S(1)} copy-done((bf16[1,768,2048]{2,1,0:T(8,128)(2,1)S(1)}, bf16[1,768,2048]{2,1,0:T(8,128)(2,1)}, u32[]{:S(2)}) %copy-start.3) | copy-done | bytes 3145752
  39.4 4.6 %shard_map.73 = (f32[64,2048]{1,0:T(8,128)S(1)}, bf16[64,2048]{1,0:T(8,128)(2,1)S(1)}, f32[64,2048]{1,0:T(8,128)S(1)}, bf16[64,2048]{1,0:T(8,128)(2,1)S(1)}) custom-call(s32[1]{0:T(128)} %bitcast.me_ref, bf16[64,2176]{1,0:T(8,128)(2,1)S(1)} %concatenate.3.a0, bf16[64,2176]{1,0:T(8,128)(2,1)S(1)} %collective-permute-done.a1, ...), custom_call_target="tpu_custom_call" | custom-call | flops 2415919104 | bytes 14680064 | tf_op jit(solution)/shard_map/pallas_call | solution.py:128
  44.7 1.5 %collective-permute-start.8 = (bf16[64,2176]{1,0:T(8,128)(2,1)S(1)}, bf16[64,2176]{1,0:T(8,128)(2,1)S(1)}, u32[]{:S(2)}, u32[]{:S(2)}) collective-permute-start(bf16[64,2176]{1,0:T(8,128)(2,1)S(1)} %collective-permute-done.6.a0), channel_id=1, source_target_pairs={{0,2},{1,3},{2,0},{3,1},{4,6},{5,7},{6,4},{7,5},{8,10},{9,11},{10,... | collective-permute-start | bytes 835592 | tf_op jit(solution)/shard_map/ppermute | solution.py:154
  47.0 6.7 %collective-permute-done.8.a2 = bf16[64,2176]{1,0:T(8,128)(2,1)S(1)} collective-permute-done((bf16[64,2176]{1,0:T(8,128)(2,1)S(1)}, bf16[64,2176]{1,0:T(8,128)(2,1)S(1)}, u32[]{:S(2)}, u32[]{:S(2)}) %collective-permute-start.8) | collective-permute-done | bytes 278560 | tf_op jit(solution)/shard_map/ppermute | solution.py:154
  54.2 4.6 %shard_map.76 = (f32[64,2048]{1,0:T(8,128)S(1)}, bf16[64,2048]{1,0:T(8,128)(2,1)S(1)}, f32[64,2048]{1,0:T(8,128)S(1)}, bf16[64,2048]{1,0:T(8,128)(2,1)S(1)}) custom-call(s32[1]{0:T(128)} %bitcast.me_ref, bf16[64,2176]{1,0:T(8,128)(2,1)S(1)} %collective-permute-done.22.a0, bf16[64,2176]{1,0:T(8,128)(2,1)S(1)} %collective-permute-done.23.a1, ...), custom_call_target="tpu_custom_call" | custom-call | flops 2415919104 | bytes 14680064 | tf_op jit(solution)/shard_map/pallas_call | solution.py:128
  58.8 1.6 %collective-permute-start.5 = (bf16[64,2048]{1,0:T(8,128)(2,1)S(1)}, bf16[64,2048]{1,0:T(8,128)(2,1)S(1)}, u32[]{:S(2)}, u32[]{:S(2)}) collective-permute-start(bf16[64,2048]{1,0:T(8,128)(2,1)S(1)} %add_convert_fusion.7), channel_id=1, source_target_pairs={{0,2},{1,3},{2,0},{3,1},{4,6},{5,7},{6,4},{7,5},{8,10},{9,11},{10,... | collective-permute-start | bytes 786440 | tf_op jit(solution)/shard_map/ppermute | solution.py:154
  60.4 4.6 %shard_map.75 = (f32[64,2048]{1,0:T(8,128)S(1)}, bf16[64,2048]{1,0:T(8,128)(2,1)S(1)}, f32[64,2048]{1,0:T(8,128)S(1)}, bf16[64,2048]{1,0:T(8,128)(2,1)S(1)}) custom-call(s32[1]{0:T(128)} %bitcast.me_ref, bf16[64,2176]{1,0:T(8,128)(2,1)S(1)} %collective-permute-done.14.a0, bf16[64,2176]{1,0:T(8,128)(2,1)S(1)} %collective-permute-done.15.a1, ...), custom_call_target="tpu_custom_call" | custom-call | flops 2415919104 | bytes 14680064 | tf_op jit(solution)/shard_map/pallas_call | solution.py:128
  65.0 0.6 collective-permute-start.26
  65.6 4.6 %shard_map.74 = (f32[64,2048]{1,0:T(8,128)S(1)}, bf16[64,2048]{1,0:T(8,128)(2,1)S(1)}, f32[64,2048]{1,0:T(8,128)S(1)}, bf16[64,2048]{1,0:T(8,128)(2,1)S(1)}) custom-call(s32[1]{0:T(128)} %bitcast.me_ref, bf16[64,2176]{1,0:T(8,128)(2,1)S(1)} %collective-permute-done.6.a0, bf16[64,2176]{1,0:T(8,128)(2,1)S(1)} %collective-permute-done.7.a1, ...), custom_call_target="tpu_custom_call" | custom-call | flops 2415919104 | bytes 14680064 | tf_op jit(solution)/shard_map/pallas_call | solution.py:128
  71.0 1.4 %collective-permute-done.11 = bf16[64,2048]{1,0:T(8,128)(2,1)S(1)} collective-permute-done((bf16[64,2048]{1,0:T(8,128)(2,1)S(1)}, bf16[64,2048]{1,0:T(8,128)(2,1)S(1)}, u32[]{:S(2)}, u32[]{:S(2)}) %collective-permute-start.11) | collective-permute-done | bytes 262176 | tf_op jit(solution)/shard_map/ppermute | solution.py:154
  73.1 7.8 %collective-permute-done.28 = bf16[64,2048]{1,0:T(8,128)(2,1)S(1)} collective-permute-done((bf16[64,2048]{1,0:T(8,128)(2,1)S(1)}, bf16[64,2048]{1,0:T(8,128)(2,1)S(1)}, u32[]{:S(2)}, u32[]{:S(2)}) %collective-permute-start.28) | collective-permute-done | bytes 262176 | tf_op jit(solution)/shard_map/ppermute | solution.py:154
  80.9 0.5 collective-permute-start.20
  81.5 1.6 %collective-permute-start.12 = (bf16[64,2048]{1,0:T(8,128)(2,1)S(1)}, bf16[64,2048]{1,0:T(8,128)(2,1)S(1)}, u32[]{:S(2)}, u32[]{:S(2)}) collective-permute-start(bf16[64,2048]{1,0:T(8,128)(2,1)S(1)} %add_convert_fusion.6), channel_id=1, source_target_pairs={{0,2},{1,3},{2,0},{3,1},{4,6},{5,7},{6,4},{7,5},{8,10},{9,11},{10,... | collective-permute-start | bytes 786440 | tf_op jit(solution)/shard_map/ppermute | solution.py:154
  83.0 7.1 %collective-permute-done.20 = bf16[64,2048]{1,0:T(8,128)(2,1)S(1)} collective-permute-done((bf16[64,2048]{1,0:T(8,128)(2,1)S(1)}, bf16[64,2048]{1,0:T(8,128)(2,1)S(1)}, u32[]{:S(2)}, u32[]{:S(2)}) %collective-permute-start.20) | collective-permute-done | bytes 262176 | tf_op jit(solution)/shard_map/ppermute | solution.py:154
  90.1 2.5 %collective-permute-start.29 = (bf16[64,2048]{1,0:T(8,128)(2,1)S(1)}, bf16[64,2048]{1,0:T(8,128)(2,1)S(1)}, u32[]{:S(2)}, u32[]{:S(2)}) collective-permute-start(bf16[64,2048]{1,0:T(8,128)(2,1)S(1)} %add_convert_fusion.1), channel_id=1, source_target_pairs={{0,12},{1,13},{2,14},{3,15},{4,8},{5,9},{6,10},{7,11},{8,4},{9,5},... | collective-permute-start | bytes 786440 | tf_op jit(solution)/shard_map/ppermute | solution.py:154
  92.7 1.4 %collective-permute-done.12 = bf16[64,2048]{1,0:T(8,128)(2,1)S(1)} collective-permute-done((bf16[64,2048]{1,0:T(8,128)(2,1)S(1)}, bf16[64,2048]{1,0:T(8,128)(2,1)S(1)}, u32[]{:S(2)}, u32[]{:S(2)}) %collective-permute-start.12) | collective-permute-done | bytes 262176 | tf_op jit(solution)/shard_map/ppermute | solution.py:154
  94.2 0.6 collective-permute-start.13
  94.8 6.3 %collective-permute-done.29 = bf16[64,2048]{1,0:T(8,128)(2,1)S(1)} collective-permute-done((bf16[64,2048]{1,0:T(8,128)(2,1)S(1)}, bf16[64,2048]{1,0:T(8,128)(2,1)S(1)}, u32[]{:S(2)}, u32[]{:S(2)}) %collective-permute-start.29) | collective-permute-done | bytes 262176 | tf_op jit(solution)/shard_map/ppermute | solution.py:154
  101.1 10.0 %collective-permute-done.21 = bf16[64,2048]{1,0:T(8,128)(2,1)S(1)} collective-permute-done((bf16[64,2048]{1,0:T(8,128)(2,1)S(1)}, bf16[64,2048]{1,0:T(8,128)(2,1)S(1)}, u32[]{:S(2)}, u32[]{:S(2)}) %collective-permute-start.21) | collective-permute-done | bytes 262176 | tf_op jit(solution)/shard_map/ppermute | solution.py:154
  111.2 0.9 add_convert_fusion
  (58 shorter events, 4.6 us)
Async XLA Ops:
  3.2 9.7 %collective-permute-start.1 = (bf16[64,2176]{1,0:T(8,128)(2,1)S(1)}, bf16[64,2176]{1,0:T(8,128)(2,1)S(1)}, u32[]{:S(2)}, u32[]{:S(2)}) collective-permute-start(bf16[64,2176]{1,0:T(8,128)(2,1)S(1)} %concatenate.3.a0), channel_id=1, source_target_pairs={{0,2},{1,3},{2,0},{3,1},{4,6},{5,7},{6,4},{7,5},{8,10},{9,11},{10,... | collective-permute-start | bytes 835592 | tf_op jit(solution)/shard_map/ppermute | solution.py:154
  6.2 11.4 %collective-permute-start.22 = (bf16[64,2176]{1,0:T(8,128)(2,1)S(1)}, bf16[64,2176]{1,0:T(8,128)(2,1)S(1)}, u32[]{:S(2)}, u32[]{:S(2)}) collective-permute-start(bf16[64,2176]{1,0:T(8,128)(2,1)S(1)} %concatenate.3.a0), channel_id=1, source_target_pairs={{0,12},{1,13},{2,14},{3,15},{4,8},{5,9},{6,10},{7,11},{8,4},{9,5},... | collective-permute-start | bytes 835592 | tf_op jit(solution)/shard_map/ppermute | solution.py:154
  9.8 23.4 %collective-permute-start.14 = (bf16[64,2176]{1,0:T(8,128)(2,1)S(1)}, bf16[64,2176]{1,0:T(8,128)(2,1)S(1)}, u32[]{:S(2)}, u32[]{:S(2)}) collective-permute-start(bf16[64,2176]{1,0:T(8,128)(2,1)S(1)} %concatenate.3.a0), channel_id=1, source_target_pairs={{0,8},{1,9},{2,10},{3,11},{4,12},{5,13},{6,14},{7,15},{8,0},{9,1},... | collective-permute-start | bytes 835592 | tf_op jit(solution)/shard_map/ppermute | solution.py:154
  9.8 24.0 %collective-permute-start = (bf16[64,2176]{1,0:T(8,128)(2,1)S(1)}, bf16[64,2176]{1,0:T(8,128)(2,1)S(1)}, u32[]{:S(2)}, u32[]{:S(2)}) collective-permute-start(bf16[64,2176]{1,0:T(8,128)(2,1)S(1)} %concatenate.3.a0), channel_id=1, source_target_pairs={{0,1},{1,0},{2,3},{3,2},{4,5},{5,4},{6,7},{7,6},{8,9},{9,8},{10,11... | collective-permute-start | bytes 835592 | tf_op jit(solution)/shard_map/ppermute | solution.py:154
  12.8 20.9 %collective-permute-start.2 = (bf16[64,2176]{1,0:T(8,128)(2,1)S(1)}, bf16[64,2176]{1,0:T(8,128)(2,1)S(1)}, u32[]{:S(2)}, u32[]{:S(2)}) collective-permute-start(bf16[64,2176]{1,0:T(8,128)(2,1)S(1)} %collective-permute-done.1.a2), channel_id=1, source_target_pairs={{0,1},{1,0},{2,3},{3,2},{4,5},{5,4},{6,7},{7,6},{8,9},{9,8},{10,11... | collective-permute-start | bytes 835592 | tf_op jit(solution)/shard_map/ppermute | solution.py:154
  12.8 31.8 %collective-permute-start.6 = (bf16[64,2176]{1,0:T(8,128)(2,1)S(1)}, bf16[64,2176]{1,0:T(8,128)(2,1)S(1)}, u32[]{:S(2)}, u32[]{:S(2)}) collective-permute-start(bf16[64,2176]{1,0:T(8,128)(2,1)S(1)} %concatenate.3.a0), channel_id=1, source_target_pairs={{0,4},{1,5},{2,6},{3,7},{4,0},{5,1},{6,2},{7,3},{8,12},{9,13},{10,... | collective-permute-start | bytes 835592 | tf_op jit(solution)/shard_map/ppermute | solution.py:154
  17.6 27.1 %collective-permute-start.24 = (bf16[64,2176]{1,0:T(8,128)(2,1)S(1)}, bf16[64,2176]{1,0:T(8,128)(2,1)S(1)}, u32[]{:S(2)}, u32[]{:S(2)}) collective-permute-start(bf16[64,2176]{1,0:T(8,128)(2,1)S(1)} %collective-permute-done.22.a0), channel_id=1, source_target_pairs={{0,2},{1,3},{2,0},{3,1},{4,6},{5,7},{6,4},{7,5},{8,10},{9,11},{10,... | collective-permute-start | bytes 835592 | tf_op jit(solution)/shard_map/ppermute | solution.py:154
  33.2 13.0 %collective-permute-start.16 = (bf16[64,2176]{1,0:T(8,128)(2,1)S(1)}, bf16[64,2176]{1,0:T(8,128)(2,1)S(1)}, u32[]{:S(2)}, u32[]{:S(2)}) collective-permute-start(bf16[64,2176]{1,0:T(8,128)(2,1)S(1)} %collective-permute-done.14.a0), channel_id=1, source_target_pairs={{0,2},{1,3},{2,0},{3,1},{4,6},{5,7},{6,4},{7,5},{8,10},{9,11},{10,... | collective-permute-start | bytes 835592 | tf_op jit(solution)/shard_map/ppermute | solution.py:154
  33.8 1.9 %copy-start = (bf16[1,2048,768]{2,1,0:T(8,128)(2,1)S(1)}, bf16[1,2048,768]{2,1,0:T(8,128)(2,1)}, u32[]{:S(2)}) copy-start(bf16[1,2048,768]{2,1,0:T(8,128)(2,1)} %gate_ref.7) | copy-start | bytes 9437188
  39.4 14.8 %copy-start.1 = (bf16[1,2048,768]{2,1,0:T(8,128)(2,1)S(1)}, bf16[1,2048,768]{2,1,0:T(8,128)(2,1)}, u32[]{:S(2)}) copy-start(bf16[1,2048,768]{2,1,0:T(8,128)(2,1)} %gate_ref.7) | copy-start | bytes 9437188
  44.0 2.3 %collective-permute-start.4 = (bf16[64,2048]{1,0:T(8,128)(2,1)S(1)}, bf16[64,2048]{1,0:T(8,128)(2,1)S(1)}, u32[]{:S(2)}, u32[]{:S(2)}) collective-permute-start(bf16[64,2048]{1,0:T(8,128)(2,1)S(1)} %get-tuple-element.24), channel_id=1, source_target_pairs={{0,1},{1,0},{2,3},{3,2},{4,5},{5,4},{6,7},{7,6},{8,9},{9,8},{10,11... | collective-permute-start | bytes 786440 | tf_op jit(solution)/shard_map/ppermute | solution.py:154
  44.1 2.6 %collective-permute-start.23 = (bf16[64,2176]{1,0:T(8,128)(2,1)S(1)}, bf16[64,2176]{1,0:T(8,128)(2,1)S(1)}, u32[]{:S(2)}, u32[]{:S(2)}) collective-permute-start(bf16[64,2176]{1,0:T(8,128)(2,1)S(1)} %collective-permute-done.22.a0), channel_id=1, source_target_pairs={{0,1},{1,0},{2,3},{3,2},{4,5},{5,4},{6,7},{7,6},{8,9},{9,8},{10,11... | collective-permute-start | bytes 835592 | tf_op jit(solution)/shard_map/ppermute | solution.py:154
  44.6 14.2 %collective-permute-start.15 = (bf16[64,2176]{1,0:T(8,128)(2,1)S(1)}, bf16[64,2176]{1,0:T(8,128)(2,1)S(1)}, u32[]{:S(2)}, u32[]{:S(2)}) collective-permute-start(bf16[64,2176]{1,0:T(8,128)(2,1)S(1)} %collective-permute-done.14.a0), channel_id=1, source_target_pairs={{0,1},{1,0},{2,3},{3,2},{4,5},{5,4},{6,7},{7,6},{8,9},{9,8},{10,11... | collective-permute-start | bytes 835592 | tf_op jit(solution)/shard_map/ppermute | solution.py:154
  44.7 9.0 %collective-permute-start.8 = (bf16[64,2176]{1,0:T(8,128)(2,1)S(1)}, bf16[64,2176]{1,0:T(8,128)(2,1)S(1)}, u32[]{:S(2)}, u32[]{:S(2)}) collective-permute-start(bf16[64,2176]{1,0:T(8,128)(2,1)S(1)} %collective-permute-done.6.a0), channel_id=1, source_target_pairs={{0,2},{1,3},{2,0},{3,1},{4,6},{5,7},{6,4},{7,5},{8,10},{9,11},{10,... | collective-permute-start | bytes 835592 | tf_op jit(solution)/shard_map/ppermute | solution.py:154
  46.2 7.5 %collective-permute-start.25 = (bf16[64,2176]{1,0:T(8,128)(2,1)S(1)}, bf16[64,2176]{1,0:T(8,128)(2,1)S(1)}, u32[]{:S(2)}, u32[]{:S(2)}) collective-permute-start(bf16[64,2176]{1,0:T(8,128)(2,1)S(1)} %collective-permute-done.24.a2), channel_id=1, source_target_pairs={{0,1},{1,0},{2,3},{3,2},{4,5},{5,4},{6,7},{7,6},{8,9},{9,8},{10,11... | collective-permute-start | bytes 835592 | tf_op jit(solution)/shard_map/ppermute | solution.py:154
  46.3 14.0 %collective-permute-start.17 = (bf16[64,2176]{1,0:T(8,128)(2,1)S(1)}, bf16[64,2176]{1,0:T(8,128)(2,1)S(1)}, u32[]{:S(2)}, u32[]{:S(2)}) collective-permute-start(bf16[64,2176]{1,0:T(8,128)(2,1)S(1)} %collective-permute-done.16.a2), channel_id=1, source_target_pairs={{0,1},{1,0},{2,3},{3,2},{4,5},{5,4},{6,7},{7,6},{8,9},{9,8},{10,11... | collective-permute-start | bytes 835592 | tf_op jit(solution)/shard_map/ppermute | solution.py:154
  46.8 18.2 %collective-permute-start.7 = (bf16[64,2176]{1,0:T(8,128)(2,1)S(1)}, bf16[64,2176]{1,0:T(8,128)(2,1)S(1)}, u32[]{:S(2)}, u32[]{:S(2)}) collective-permute-start(bf16[64,2176]{1,0:T(8,128)(2,1)S(1)} %collective-permute-done.6.a0), channel_id=1, source_target_pairs={{0,1},{1,0},{2,3},{3,2},{4,5},{5,4},{6,7},{7,6},{8,9},{9,8},{10,11... | collective-permute-start | bytes 835592 | tf_op jit(solution)/shard_map/ppermute | solution.py:154
  53.7 41.1 %collective-permute-start.3 = (bf16[64,2048]{1,0:T(8,128)(2,1)S(1)}, bf16[64,2048]{1,0:T(8,128)(2,1)S(1)}, u32[]{:S(2)}, u32[]{:S(2)}) collective-permute-start(bf16[64,2048]{1,0:T(8,128)(2,1)S(1)} %get-tuple-element.22), channel_id=1, source_target_pairs={{0,1},{1,0},{2,3},{3,2},{4,5},{5,4},{6,7},{7,6},{8,9},{9,8},{10,11... | collective-permute-start | bytes 786440 | tf_op jit(solution)/shard_map/ppermute | solution.py:154
  53.7 11.9 %collective-permute-start.9 = (bf16[64,2176]{1,0:T(8,128)(2,1)S(1)}, bf16[64,2176]{1,0:T(8,128)(2,1)S(1)}, u32[]{:S(2)}, u32[]{:S(2)}) collective-permute-start(bf16[64,2176]{1,0:T(8,128)(2,1)S(1)} %collective-permute-done.8.a2), channel_id=1, source_target_pairs={{0,1},{1,0},{2,3},{3,2},{4,5},{5,4},{6,7},{7,6},{8,9},{9,8},{10,11... | collective-permute-start | bytes 835592 | tf_op jit(solution)/shard_map/ppermute | solution.py:154
  58.8 36.0 %collective-permute-start.5 = (bf16[64,2048]{1,0:T(8,128)(2,1)S(1)}, bf16[64,2048]{1,0:T(8,128)(2,1)S(1)}, u32[]{:S(2)}, u32[]{:S(2)}) collective-permute-start(bf16[64,2048]{1,0:T(8,128)(2,1)S(1)} %add_convert_fusion.7), channel_id=1, source_target_pairs={{0,2},{1,3},{2,0},{3,1},{4,6},{5,7},{6,4},{7,5},{8,10},{9,11},{10,... | collective-permute-start | bytes 786440 | tf_op jit(solution)/shard_map/ppermute | solution.py:154
  60.4 9.9 %collective-permute-start.27 = (bf16[64,2048]{1,0:T(8,128)(2,1)S(1)}, bf16[64,2048]{1,0:T(8,128)(2,1)S(1)}, u32[]{:S(2)}, u32[]{:S(2)}) collective-permute-start(bf16[64,2048]{1,0:T(8,128)(2,1)S(1)} %get-tuple-element.36), channel_id=1, source_target_pairs={{0,1},{1,0},{2,3},{3,2},{4,5},{5,4},{6,7},{7,6},{8,9},{9,8},{10,11... | collective-permute-start | bytes 786440 | tf_op jit(solution)/shard_map/ppermute | solution.py:154
  65.0 8.0 %collective-permute-start.26 = (bf16[64,2048]{1,0:T(8,128)(2,1)S(1)}, bf16[64,2048]{1,0:T(8,128)(2,1)S(1)}, u32[]{:S(2)}, u32[]{:S(2)}) collective-permute-start(bf16[64,2048]{1,0:T(8,128)(2,1)S(1)} %get-tuple-element.34), channel_id=1, source_target_pairs={{0,1},{1,0},{2,3},{3,2},{4,5},{5,4},{6,7},{7,6},{8,9},{9,8},{10,11... | collective-permute-start | bytes 786440 | tf_op jit(solution)/shard_map/ppermute | solution.py:154
  65.6 5.2 %collective-permute-start.19 = (bf16[64,2048]{1,0:T(8,128)(2,1)S(1)}, bf16[64,2048]{1,0:T(8,128)(2,1)S(1)}, u32[]{:S(2)}, u32[]{:S(2)}) collective-permute-start(bf16[64,2048]{1,0:T(8,128)(2,1)S(1)} %get-tuple-element.32), channel_id=1, source_target_pairs={{0,1},{1,0},{2,3},{3,2},{4,5},{5,4},{6,7},{7,6},{8,9},{9,8},{10,11... | collective-permute-start | bytes 786440 | tf_op jit(solution)/shard_map/ppermute | solution.py:154
  70.2 11.2 %collective-permute-start.18 = (bf16[64,2048]{1,0:T(8,128)(2,1)S(1)}, bf16[64,2048]{1,0:T(8,128)(2,1)S(1)}, u32[]{:S(2)}, u32[]{:S(2)}) collective-permute-start(bf16[64,2048]{1,0:T(8,128)(2,1)S(1)} %get-tuple-element.30), channel_id=1, source_target_pairs={{0,1},{1,0},{2,3},{3,2},{4,5},{5,4},{6,7},{7,6},{8,9},{9,8},{10,11... | collective-permute-start | bytes 786440 | tf_op jit(solution)/shard_map/ppermute | solution.py:154
  70.8 1.6 %collective-permute-start.11 = (bf16[64,2048]{1,0:T(8,128)(2,1)S(1)}, bf16[64,2048]{1,0:T(8,128)(2,1)S(1)}, u32[]{:S(2)}, u32[]{:S(2)}) collective-permute-start(bf16[64,2048]{1,0:T(8,128)(2,1)S(1)} %get-tuple-element.28), channel_id=1, source_target_pairs={{0,1},{1,0},{2,3},{3,2},{4,5},{5,4},{6,7},{7,6},{8,9},{9,8},{10,11... | collective-permute-start | bytes 786440 | tf_op jit(solution)/shard_map/ppermute | solution.py:154
  72.4 8.5 %collective-permute-start.28 = (bf16[64,2048]{1,0:T(8,128)(2,1)S(1)}, bf16[64,2048]{1,0:T(8,128)(2,1)S(1)}, u32[]{:S(2)}, u32[]{:S(2)}) collective-permute-start(bf16[64,2048]{1,0:T(8,128)(2,1)S(1)} %add_convert_fusion.2), channel_id=1, source_target_pairs={{0,2},{1,3},{2,0},{3,1},{4,6},{5,7},{6,4},{7,5},{8,10},{9,11},{10,... | collective-permute-start | bytes 786440 | tf_op jit(solution)/shard_map/ppermute | solution.py:154
  73.0 19.7 %collective-permute-start.10 = (bf16[64,2048]{1,0:T(8,128)(2,1)S(1)}, bf16[64,2048]{1,0:T(8,128)(2,1)S(1)}, u32[]{:S(2)}, u32[]{:S(2)}) collective-permute-start(bf16[64,2048]{1,0:T(8,128)(2,1)S(1)} %get-tuple-element.26), channel_id=1, source_target_pairs={{0,1},{1,0},{2,3},{3,2},{4,5},{5,4},{6,7},{7,6},{8,9},{9,8},{10,11... | collective-permute-start | bytes 786440 | tf_op jit(solution)/shard_map/ppermute | solution.py:154
  80.9 9.2 %collective-permute-start.20 = (bf16[64,2048]{1,0:T(8,128)(2,1)S(1)}, bf16[64,2048]{1,0:T(8,128)(2,1)S(1)}, u32[]{:S(2)}, u32[]{:S(2)}) collective-permute-start(bf16[64,2048]{1,0:T(8,128)(2,1)S(1)} %add_convert_fusion.4), channel_id=1, source_target_pairs={{0,2},{1,3},{2,0},{3,1},{4,6},{5,7},{6,4},{7,5},{8,10},{9,11},{10,... | collective-permute-start | bytes 786440 | tf_op jit(solution)/shard_map/ppermute | solution.py:154
  81.5 12.6 %collective-permute-start.12 = (bf16[64,2048]{1,0:T(8,128)(2,1)S(1)}, bf16[64,2048]{1,0:T(8,128)(2,1)S(1)}, u32[]{:S(2)}, u32[]{:S(2)}) collective-permute-start(bf16[64,2048]{1,0:T(8,128)(2,1)S(1)} %add_convert_fusion.6), channel_id=1, source_target_pairs={{0,2},{1,3},{2,0},{3,1},{4,6},{5,7},{6,4},{7,5},{8,10},{9,11},{10,... | collective-permute-start | bytes 786440 | tf_op jit(solution)/shard_map/ppermute | solution.py:154
  90.1 11.0 %collective-permute-start.29 = (bf16[64,2048]{1,0:T(8,128)(2,1)S(1)}, bf16[64,2048]{1,0:T(8,128)(2,1)S(1)}, u32[]{:S(2)}, u32[]{:S(2)}) collective-permute-start(bf16[64,2048]{1,0:T(8,128)(2,1)S(1)} %add_convert_fusion.1), channel_id=1, source_target_pairs={{0,12},{1,13},{2,14},{3,15},{4,8},{5,9},{6,10},{7,11},{8,4},{9,5},... | collective-permute-start | bytes 786440 | tf_op jit(solution)/shard_map/ppermute | solution.py:154
  92.7 18.5 %collective-permute-start.21 = (bf16[64,2048]{1,0:T(8,128)(2,1)S(1)}, bf16[64,2048]{1,0:T(8,128)(2,1)S(1)}, u32[]{:S(2)}, u32[]{:S(2)}) collective-permute-start(bf16[64,2048]{1,0:T(8,128)(2,1)S(1)} %add_convert_fusion.3), channel_id=1, source_target_pairs={{0,8},{1,9},{2,10},{3,11},{4,12},{5,13},{6,14},{7,15},{8,0},{9,1},... | collective-permute-start | bytes 786440 | tf_op jit(solution)/shard_map/ppermute | solution.py:154
  94.2 17.0 %collective-permute-start.13 = (bf16[64,2048]{1,0:T(8,128)(2,1)S(1)}, bf16[64,2048]{1,0:T(8,128)(2,1)S(1)}, u32[]{:S(2)}, u32[]{:S(2)}) collective-permute-start(bf16[64,2048]{1,0:T(8,128)(2,1)S(1)} %add_convert_fusion.5), channel_id=1, source_target_pairs={{0,4},{1,5},{2,6},{3,7},{4,0},{5,1},{6,2},{7,3},{8,12},{9,13},{10,... | collective-permute-start | bytes 786440 | tf_op jit(solution)/shard_map/ppermute | solution.py:154
  (2 other events, 3.8 us)

commit v2 on v0

--- a/solution.py
+++ b/solution.py
@@ -1,7 +1,47 @@
+import functools
+
 import jax
 import jax.numpy as jnp
 from jax import lax
+from jax.experimental import pallas as pl
+from jax.experimental.pallas import tpu as pltpu
 from jax.sharding import PartitionSpec as P
+
+LANES = 128
+CHUNK = 256
+STEPS = [
+    ('A4', []),
+    ('A8', []),
+    ('A2', []),
+    ('A1', []),
+    ('A3', []),
+    ('A12', []),
+    ('A6', []),
+    ('A5', []),
+    ('A7', []),
+    ('A10', []),
+    ('A9', []),
+    ('A11', []),
+    ('A14', []),
+    ('A13', []),
+    ('A15', []),
+    ('K0', []),
+    ('O0', []),
+    ('X0', []),
+    ('K4', []),
+    ('O4', []),
+    ('X4', []),
+    ('K8', []),
+    ('O8', []),
+    ('X8', []),
+    ('K12', []),
+    ('O12', []),
+    ('X12', []),
+    ('Z4', []),
+    ('Z8', []),
+    ('Z12', []),
+]
+VMEM_LIMIT = 24 * 2**20
 
 
 def dequantize(values, scales):
@@ -22,7 +62,7 @@
     )
 
 
-def on_device(tokens, scales, expert_ids, gate_weights, w_gate, w_up, w_down):
+def routed(tokens, scales, expert_ids, gate_weights, w_gate, w_up, w_down):
     peer_count = lax.axis_size("expert")
     token_count, feature_width = tokens.shape
     top_count = expert_ids.shape[1]
@@ -63,6 +103,172 @@
     return combined.astype(jnp.bfloat16)
 
 
+def pack_kernel(expert_total, *refs):
+    sources, out_ref, targets, sems = refs[:4], refs[4], refs[5:9], refs[9]
+    tokens_ref, scales_ref, ids_ref, weights_ref = targets
+    copies = [
+        pltpu.make_async_copy(source, target, sems.at[index])
+        for index, (source, target) in enumerate(zip(sources, targets, strict=True))
+    ]
+    for copy in copies:
+        copy.start()
+    count, width = tokens_ref.shape
+    blocks = scales_ref.shape[0]
+    size = width // blocks
+    packed = out_ref.shape[1]
+    square = (count, count)
+    same = lax.broadcasted_iota(jnp.int32, square, 0) == lax.broadcasted_iota(jnp.int32, square, 1)
+    same = same.astype(jnp.float32).astype(jnp.bfloat16)
+
+    def turn(values):
+        return lax.dot_general(
+            same, values, (((1,), (1,)), ((), ())), preferred_element_type=jnp.float32
+        )
+
+    for copy in copies[1:]:
+        copy.wait()
+    line = lax.broadcasted_iota(jnp.int32, (packed - width, count), 0)
+    dense = jnp.zeros(line.shape, jnp.float32)
+    for k in range(ids_ref.shape[0]):
+        dense += jnp.where(line % expert_total == ids_ref[k : k + 1, :], weights_ref[k : k + 1, :], 0.0)
+    terms = jnp.zeros(line.shape, jnp.float32)
+    for index in range(3):
+        term = dense.astype(jnp.bfloat16).astype(jnp.float32)
+        terms = jnp.where(line // expert_total == index, term, terms)
+        dense = dense - term
+    out_ref[:, width:] = turn(terms.astype(jnp.bfloat16)).astype(jnp.bfloat16)
+    scales = turn(scales_ref[...])
+    copies[0].wait()
+    for block in range(blocks):
+        columns = slice(block * size, (block + 1) * size)
+        values = tokens_ref[:, columns].astype(jnp.float32) * scales[:, block : block + 1]
+        out_ref[:, columns] = values.astype(jnp.bfloat16)
+
+
+def pack_rows(tokens, scales, expert_ids, gate_weights, expert_total):
+    count, width = tokens.shape
+    packed = width + -(-3 * expert_total // LANES) * LANES
+    arrays = (tokens, scales.T, expert_ids.T, gate_weights.T)
+    return pl.pallas_call(
+        functools.partial(pack_kernel, expert_total),
+        in_specs=[pl.BlockSpec(memory_space=pl.ANY)] * 4,
+        out_specs=pl.BlockSpec(memory_space=pltpu.VMEM),
+        out_shape=jax.ShapeDtypeStruct((count, packed), jnp.bfloat16),
+        scratch_shapes=[pltpu.VMEM(array.shape, array.dtype) for array in arrays]
+        + [pltpu.SemaphoreType.DMA((4,))],
+        compiler_params=pltpu.CompilerParams(vmem_limit_bytes=64 * 2**20),
+        cost_estimate=pl.CostEstimate(flops=1, bytes_accessed=1, transcendentals=0),
+    )(*arrays)
+
+
+def experts_on(expert_total, me_ref, blocks, outs, gate_ref, up_ref, down_ref, hidden_ref):
+    hidden_width, width = down_ref.shape[1:]
+    inputs = jnp.concatenate([block[:, :width] for block in blocks], axis=0)
+    for index in range(hidden_width // CHUNK):
+        columns = slice(index * CHUNK, (index + 1) * CHUNK)
+        gate_part = jnp.dot(inputs, gate_ref[0, :, columns], preferred_element_type=jnp.float32)
+        up_part = jnp.dot(inputs, up_ref[0, :, columns], preferred_element_type=jnp.float32)
+        hidden = gate_part / (1.0 + jnp.exp(-gate_part)) * up_part
+        hidden_ref[:, columns] = hidden.astype(jnp.bfloat16)
+    factors = []
+    for block in blocks:
+        terms = block[:, width:].astype(jnp.float32)
+        lane = lax.broadcasted_iota(jnp.int32, terms.shape, 1) % expert_total
+        factors.append(jnp.sum(jnp.where(lane == me_ref[0], terms, 0.0), axis=1, keepdims=True))
+    factor = jnp.concatenate(factors, axis=0)
+    hidden = hidden_ref[...]
+    for start in range(0, width, 512):
+        columns = slice(start, start + 512)
+        result = jnp.dot(hidden, down_ref[0, :, columns], preferred_element_type=jnp.float32)
+        result = factor * result.astype(jnp.bfloat16).astype(jnp.float32)
+        row = 0
+        for out in outs:
+            out[:, columns] = result[row : row + out.shape[0], :].astype(out.dtype)
+            row += out.shape[0]
+
+
+def expert_kernel(expert_total, number, *refs):
+    me_ref, blocks, weights, outs, hidden_ref = refs[0], refs[1 : 1 + number], refs[1 + number : 4 + number], refs[-4:-1], refs[-1]
+    experts_on(expert_total, me_ref, blocks, outs, *weights, hidden_ref)
+
+
+def weighted_outputs(expert_total, me, blocks, weights):
+    count = blocks[0].shape[0]
+    rows = sum(block.shape[0] for block in blocks)
+    hidden_width, width = weights[2].shape[1:]
+    vmem = pl.BlockSpec(memory_space=pltpu.VMEM)
+    return pl.pallas_call(
+        functools.partial(expert_kernel, expert_total, len(blocks)),
+        in_specs=[pl.BlockSpec(memory_space=pltpu.SMEM)] + [vmem] * (len(blocks) + 3),
+        out_specs=[vmem] * 3,
+        out_shape=[
+            jax.ShapeDtypeStruct((count, width), jnp.float32),
+            jax.ShapeDtypeStruct((count, width), jnp.float32),
+            jax.ShapeDtypeStruct((rows - 2 * count, width), jnp.bfloat16),
+        ],
+        scratch_shapes=[pltpu.VMEM((rows, hidden_width), jnp.bfloat16)],
+        compiler_params=pltpu.CompilerParams(vmem_limit_bytes=VMEM_LIMIT),
+        cost_estimate=pl.CostEstimate(flops=1, bytes_accessed=1, transcendentals=0),
+    )(me, *blocks, *weights)
+
+
+def gathered(tokens, scales, expert_ids, gate_weights, w_gate, w_up, w_down):
+    peer_count = lax.axis_size("expert")
+
+    def exchange(array, mask):
+        return lax.ppermute(array, "expert", [(i, i ^ mask) for i in range(peer_count)])
+
+    def after(array, names):
+        if not names:
+            return array
+        return lax.optimization_barrier((array,) + tuple(done[name] for name in names))[0]
+
+    me = lax.axis_index("expert").astype(jnp.int32).reshape(1)
+    weights = (w_gate, w_up, w_down)
+    done = {"A0": pack_rows(tokens, scales, expert_ids, gate_weights, peer_count)}
+    own, other, sums = {}, {}, {}
+    for step, ties in STEPS:
+        kind, number = step[0], int(step[1:])
+        if kind == "A":
+            bit = number & -number if number % 4 else 1 << (number.bit_length() - 1)
+            done[step] = exchange(after(done["A%d" % (number - bit)], ties), bit)
+        elif kind == "B":
+            pair = jnp.concatenate([done["A%d" % number], done["A%d" % (number + 2)]], axis=0)
+            done[step] = exchange(after(pair, ties), 1)
+        elif kind == "K":
+            names = ["A%d" % number, "A%d" % (number + 2)]
+            names += ["B%d" % number] if "B%d" % number in done else ["A%d" % (number + 1), "A%d" % (number + 3)]
+            blocks = [done[name] for name in names]
+            blocks[0] = after(blocks[0], ties)
+            parts = weighted_outputs(peer_count, me, blocks, weights)
+            done[step] = parts[0]
+            own[number], other[number] = parts[:2], parts[2]
+        elif kind == "O":
+            got = exchange(other[number], 1).astype(jnp.float32)
+            count = got.shape[0] // 2
+            done[step] = (own[number][1] + got[count:]).astype(jnp.bfloat16)
+            own[number] = own[number][0] + got[:count]
+        elif kind == "X":
+            done[step] = exchange(after(done["O%d" % number], ties), 2)
+            sums[number] = own[number] + done[step].astype(jnp.float32)
+        elif kind == "Z":
+            done[step] = exchange(after(sums[number].astype(jnp.bfloat16), ties), number)
+    combined = sums[0]
+    for z in range(4, peer_count, 4):
+        combined = combined + done["Z%d" % z].astype(jnp.float32)
+    return combined.astype(jnp.bfloat16)
+
+
+def on_device(tokens, scales, expert_ids, gate_weights, w_gate, w_up, w_down):
+    peer_count = lax.axis_size("expert")
+    local_experts = w_gate.shape[0]
+    capacity = 2 * tokens.shape[0] * expert_ids.shape[1] // (peer_count * local_experts)
+    power_of_two = peer_count & (peer_count - 1) == 0
+    whole = capacity >= tokens.shape[0] and local_experts == 1 and peer_count >= 4 and power_of_two
+    layer = gathered if whole else routed
+    return layer(tokens, scales, expert_ids, gate_weights, w_gate, w_up, w_down)
+
+
 def solution(mesh):
     return jax.shard_map(
         on_device,

time: 261 us -> 89.3 us (0.34)
  waiting for transfers between devices: 165 us -> 43.3 us
  local copies, waits for them, and re-layouts: 43.7 us -> 6.63 us
  matrix products: 24.2 us -> 0 us
  Pallas kernels: 0 us -> 12.7 us
  starting transfers between devices: 19 us -> 24.3 us
  other arithmetic: 6.16 us -> 1.83 us
    all_to_all x3 -> x0, waiting for transfers between devices: 165 us -> none  [the longest x1 90.7 us: on_device(): lax.all_to_all(outputs, 'expert', split_axis=0, concat_axis=0, tiled=True)]
    ppermute x0 -> x26, waiting for transfers between devices: none -> 43.3 us  [exchange(): lax.ppermute(array, 'expert', [(i, i ^ mask) for i in range(peer_count)])]
    ppermute x0 -> x26, starting transfers between devices: none -> 24.3 us  [exchange(): lax.ppermute(array, 'expert', [(i, i ^ mask) for i in range(peer_count)])]
    dot_general x2 -> x0, matrix products: 24.2 us -> none  [the longest x1 13.5 us: apply_experts(): jnp.einsum('pecf,efd->pecd', hidden, w_down, preferred_element_type=jnp.f...]
    all_to_all x3 -> x0, starting transfers between devices: 19 us -> none  [the longest x1 6.69 us: on_device(): lax.all_to_all(outputs, 'expert', split_axis=0, concat_axis=0, tiled=True)]
    mul x5 -> x0, local copies, waits for them, and re-layouts: 16.3 us -> none  [the longest x3 16.1 us: dequantize(): values.astype(jnp.float32).reshape(split_shape)]
    scatter x2 -> x0, local copies, waits for them, and re-layouts: 16.2 us -> none  [the longest x1 13.2 us: on_device(): send_values = jnp.zeros((expert_total * capacity, feature_width), jnp.bfl...]
    pallas_call x0 -> x5, Pallas kernels: none -> 12.7 us  [the longest x4 10.7 us: weighted_outputs(): pl.pallas_call(functools.partial(expert_kernel, expert_total, len(blocks)...]
  transfers between devices with their start and end apart: 3 -> 26, of which waited for: 2 -> 10; matrix products, arithmetic and copies ran while one was open for 11% -> 1% of each run, Pallas kernels for 0% -> 12%
where the time goes in v2:
time: 89.3 us; the launch traced here: 88.8 us
  waiting for transfers between devices  43.3 us (48%)
  starting transfers between devices  24.3 us (27%)
  Pallas kernels  12.7 us (14%)
  local copies, waits for them, and re-layouts  6.63 us (7%)
  other arithmetic  1.83 us (2%)
    ppermute x26, waiting for transfers between devices, exchange(): lax.ppermute(array, 'expert', [(i, i ^ mask) for i in range(peer_count)])  43.3 us
    ppermute x26, starting transfers between devices, exchange(): lax.ppermute(array, 'expert', [(i, i ^ mask) for i in range(peer_count)])  24.3 us
    pallas_call x4, Pallas kernels, weighted_outputs(): pl.pallas_call(functools.partial(expert_kernel, expert_total, len(blocks)...  10.7 us
    unnamed x14, local copies, waits for them, and re-layouts  6.63 us
    pallas_call x1, Pallas kernels, pack_rows(): pl.pallas_call(functools.partial(pack_kernel, expert_total), in_specs=[pl...  1.94 us
  transfers between devices with their start and end apart: 26, of which 10 were waited for; matrix products, arithmetic and copies ran while one was open for 1% of the time, Pallas kernels for 12%

profile of v2, /device:TPU:12, one launch (start us, length us, event | category | flops | bytes accessed | tf_op | source)
XLA Modules:
  0.0 88.8 jit_solution(7586416079557590844)
XLA Ops:
  0.0 1.9 %shard_map.73.refs_1_ = bf16[64,2176]{1,0:T(8,128)(2,1)} custom-call(bf16[64,2048]{1,0:T(8,128)(2,1)} %refs_0_.1, bf16[16,64]{1,0:T(8,128)(2,1)} %bitcast.4, s32[8,64]{1,0:T(8,128)} %bitcast.5, f32[8,64]{1,0:T(8,128)} %bitcast.6), custom_call_target="tpu_custom_call" | custom-call | flops 1 | bytes 1 | tf_op jit(solution)/shard_map/pallas_call | solution.py:152
  1.9 1.6 %collective-permute-start = (bf16[64,2176]{1,0:T(8,128)(2,1)}, bf16[64,2176]{1,0:T(8,128)(2,1)S(1)}, u32[]{:S(2)}, u32[]{:S(2)}) collective-permute-start(bf16[64,2176]{1,0:T(8,128)(2,1)} %shard_map.73.refs_1_), channel_id=1, source_target_pairs={{0,2},{1,3},{2,0},{3,1},{4,6},{5,7},{6,4},{7,5},{8,10},{9,11},{10,... | collective-permute-start | bytes 835592 | tf_op jit(solution)/shard_map/ppermute | solution.py:219
  4.0 2.6 %collective-permute-start.12 = (bf16[64,2176]{1,0:T(8,128)(2,1)}, bf16[64,2176]{1,0:T(8,128)(2,1)S(1)}, u32[]{:S(2)}, u32[]{:S(2)}) collective-permute-start(bf16[64,2176]{1,0:T(8,128)(2,1)} %shard_map.73.refs_1_), channel_id=1, source_target_pairs={{0,8},{1,9},{2,10},{3,11},{4,12},{5,13},{6,14},{7,15},{8,0},{9,1},... | collective-permute-start | bytes 835592 | tf_op jit(solution)/shard_map/ppermute | solution.py:219
  6.5 4.1 %collective-permute-done.refs_2_ = bf16[64,2176]{1,0:T(8,128)(2,1)S(1)} collective-permute-done((bf16[64,2176]{1,0:T(8,128)(2,1)}, bf16[64,2176]{1,0:T(8,128)(2,1)S(1)}, u32[]{:S(2)}, u32[]{:S(2)}) %collective-permute-start) | collective-permute-done | bytes 278560 | tf_op jit(solution)/shard_map/ppermute | solution.py:219
  10.6 5.1 %collective-permute-done.5.refs_1_ = bf16[64,2176]{1,0:T(8,128)(2,1)S(1)} collective-permute-done((bf16[64,2176]{1,0:T(8,128)(2,1)}, bf16[64,2176]{1,0:T(8,128)(2,1)S(1)}, u32[]{:S(2)}, u32[]{:S(2)}) %collective-permute-start.5) | collective-permute-done | bytes 278560 | tf_op jit(solution)/shard_map/ppermute | solution.py:219
  15.7 0.5 collective-permute-start.6
  16.3 2.6 %collective-permute-done.12.refs_1_ = bf16[64,2176]{1,0:T(8,128)(2,1)S(1)} collective-permute-done((bf16[64,2176]{1,0:T(8,128)(2,1)}, bf16[64,2176]{1,0:T(8,128)(2,1)S(1)}, u32[]{:S(2)}, u32[]{:S(2)}) %collective-permute-start.12) | collective-permute-done | bytes 278560 | tf_op jit(solution)/shard_map/ppermute | solution.py:219
  18.9 0.5 collective-permute-start.13
  19.5 2.6 %collective-permute-start.19 = (bf16[64,2176]{1,0:T(8,128)(2,1)S(1)}, bf16[64,2176]{1,0:T(8,128)(2,1)S(1)}, u32[]{:S(2)}, u32[]{:S(2)}) collective-permute-start(bf16[64,2176]{1,0:T(8,128)(2,1)S(1)} %collective-permute-done.5.refs_1_), channel_id=1, source_target_pairs={{0,8},{1,9},{2,10},{3,11},{4,12},{5,13},{6,14},{7,15},{8,0},{9,1},... | collective-permute-start | bytes 835592 | tf_op jit(solution)/shard_map/ppermute | solution.py:219
  22.0 1.9 %copy-done = bf16[1,2048,768]{2,1,0:T(8,128)(2,1)S(1)} copy-done((bf16[1,2048,768]{2,1,0:T(8,128)(2,1)S(1)}, bf16[1,2048,768]{2,1,0:T(8,128)(2,1)}, u32[]{:S(2)}) %copy-start) | copy-done | bytes 3145752
  23.9 1.9 %copy-done.2 = bf16[1,2048,768]{2,1,0:T(8,128)(2,1)S(1)} copy-done((bf16[1,2048,768]{2,1,0:T(8,128)(2,1)S(1)}, bf16[1,2048,768]{2,1,0:T(8,128)(2,1)}, u32[]{:S(2)}) %copy-start.2) | copy-done | bytes 3145752
  25.8 1.9 %copy-done.4 = bf16[1,768,2048]{2,1,0:T(8,128)(2,1)S(1)} copy-done((bf16[1,768,2048]{2,1,0:T(8,128)(2,1)S(1)}, bf16[1,768,2048]{2,1,0:T(8,128)(2,1)}, u32[]{:S(2)}) %copy-start.4) | copy-done | bytes 3145752
  27.7 1.0 %copy-done.6 = bf16[64,2176]{1,0:T(8,128)(2,1)S(1)} copy-done((bf16[64,2176]{1,0:T(8,128)(2,1)S(1)}, bf16[64,2176]{1,0:T(8,128)(2,1)}, u32[]{:S(2)}) %copy-start.6) | copy-done | bytes 278552
  28.7 2.7 %shard_map.74 = (f32[64,2048]{1,0:T(8,128)S(1)}, f32[64,2048]{1,0:T(8,128)S(1)}, bf16[128,2048]{1,0:T(8,128)(2,1)S(1)}) custom-call(s32[1]{0:T(128)} %bitcast.refs_0_, bf16[64,2176]{1,0:T(8,128)(2,1)S(1)} %copy-done.6, bf16[64,2176]{1,0:T(8,128)(2,1)S(1)} %collective-permute-done.refs_2_, bf16[64,2176]{1,0:T(8,128)(2,1)S(1)} %collective-permute-done.1.refs_3_, ...), custom_call_target="tpu_custom_call" | custom-call | flops 1 | bytes 1 | tf_op jit(solution)/shard_map/pallas_call | solution.py:200
  32.6 1.4 %collective-permute-start.20 = (bf16[64,2176]{1,0:T(8,128)(2,1)S(1)}, bf16[64,2176]{1,0:T(8,128)(2,1)S(1)}, u32[]{:S(2)}, u32[]{:S(2)}) collective-permute-start(bf16[64,2176]{1,0:T(8,128)(2,1)S(1)} %collective-permute-done.19.refs_1_), channel_id=1, source_target_pairs={{0,2},{1,3},{2,0},{3,1},{4,6},{5,7},{6,4},{7,5},{8,10},{9,11},{10,... | collective-permute-start | bytes 835592 | tf_op jit(solution)/shard_map/ppermute | solution.py:219
  34.0 2.7 %shard_map.75 = (f32[64,2048]{1,0:T(8,128)S(1)}, f32[64,2048]{1,0:T(8,128)S(1)}, bf16[128,2048]{1,0:T(8,128)(2,1)S(1)}) custom-call(s32[1]{0:T(128)} %bitcast.refs_0_, bf16[64,2176]{1,0:T(8,128)(2,1)S(1)} %collective-permute-done.5.refs_1_, bf16[64,2176]{1,0:T(8,128)(2,1)S(1)} %collective-permute-done.6.refs_2_, ...), custom_call_target="tpu_custom_call" | custom-call | flops 1 | bytes 1 | tf_op jit(solution)/shard_map/pallas_call | solution.py:200
  37.2 2.7 %shard_map.76 = (f32[64,2048]{1,0:T(8,128)S(1)}, f32[64,2048]{1,0:T(8,128)S(1)}, bf16[128,2048]{1,0:T(8,128)(2,1)S(1)}) custom-call(s32[1]{0:T(128)} %bitcast.refs_0_, bf16[64,2176]{1,0:T(8,128)(2,1)S(1)} %collective-permute-done.12.refs_1_, bf16[64,2176]{1,0:T(8,128)(2,1)S(1)} %collective-permute-done.13.refs_2_, ...), custom_call_target="tpu_custom_call" | custom-call | flops 1 | bytes 1 | tf_op jit(solution)/shard_map/pallas_call | solution.py:200
  40.1 1.1 %collective-permute-done.20.refs_2_ = bf16[64,2176]{1,0:T(8,128)(2,1)S(1)} collective-permute-done((bf16[64,2176]{1,0:T(8,128)(2,1)S(1)}, bf16[64,2176]{1,0:T(8,128)(2,1)S(1)}, u32[]{:S(2)}, u32[]{:S(2)}) %collective-permute-start.20) | collective-permute-done | bytes 278560 | tf_op jit(solution)/shard_map/ppermute | solution.py:219
  41.3 1.5 %collective-permute-start.4 = (bf16[64,2048]{1,0:T(8,128)(2,1)S(1)}, bf16[64,2048]{1,0:T(8,128)(2,1)S(1)}, u32[]{:S(2)}, u32[]{:S(2)}) collective-permute-start(bf16[64,2048]{1,0:T(8,128)(2,1)S(1)} %fusion.9), channel_id=1, source_target_pairs={{0,2},{1,3},{2,0},{3,1},{4,6},{5,7},{6,4},{7,5},{8,10},{9,11},{10,... | collective-permute-start | bytes 786440 | tf_op jit(solution)/shard_map/ppermute | solution.py:219
  42.9 2.7 %shard_map.77 = (f32[64,2048]{1,0:T(8,128)S(1)}, f32[64,2048]{1,0:T(8,128)S(1)}, bf16[128,2048]{1,0:T(8,128)(2,1)S(1)}) custom-call(s32[1]{0:T(128)} %bitcast.refs_0_, bf16[64,2176]{1,0:T(8,128)(2,1)S(1)} %collective-permute-done.19.refs_1_, bf16[64,2176]{1,0:T(8,128)(2,1)S(1)} %collective-permute-done.20.refs_2_, ...), custom_call_target="tpu_custom_call" | custom-call | flops 1 | bytes 1 | tf_op jit(solution)/shard_map/pallas_call | solution.py:200
  46.0 1.3 %collective-permute-start.10 = (bf16[64,2048]{1,0:T(8,128)(2,1)S(1)}, bf16[64,2048]{1,0:T(8,128)(2,1)S(1)}, u32[]{:S(2)}, u32[]{:S(2)}) collective-permute-start(bf16[64,2048]{1,0:T(8,128)(2,1)S(1)} %fusion.6), channel_id=1, source_target_pairs={{0,2},{1,3},{2,0},{3,1},{4,6},{5,7},{6,4},{7,5},{8,10},{9,11},{10,... | collective-permute-start | bytes 786440 | tf_op jit(solution)/shard_map/ppermute | solution.py:219
  47.5 0.9 collective-permute-start.17
  48.4 7.8 %collective-permute-done.10 = bf16[64,2048]{1,0:T(8,128)(2,1)S(1)} collective-permute-done((bf16[64,2048]{1,0:T(8,128)(2,1)S(1)}, bf16[64,2048]{1,0:T(8,128)(2,1)S(1)}, u32[]{:S(2)}, u32[]{:S(2)}) %collective-permute-start.10) | collective-permute-done | bytes 262176 | tf_op jit(solution)/shard_map/ppermute | solution.py:219
  56.2 3.2 %collective-permute-start.11 = (bf16[64,2048]{1,0:T(8,128)(2,1)S(1)}, bf16[64,2048]{1,0:T(8,128)(2,1)S(1)}, u32[]{:S(2)}, u32[]{:S(2)}) collective-permute-start(bf16[64,2048]{1,0:T(8,128)(2,1)S(1)} %fusion.8), channel_id=1, source_target_pairs={{0,4},{1,5},{2,6},{3,7},{4,0},{5,1},{6,2},{7,3},{8,12},{9,13},{10,... | collective-permute-start | bytes 786440 | tf_op jit(solution)/shard_map/ppermute | solution.py:219
  59.5 0.6 collective-permute-start.24
  60.1 1.2 %collective-permute-done.17 = bf16[64,2048]{1,0:T(8,128)(2,1)S(1)} collective-permute-done((bf16[64,2048]{1,0:T(8,128)(2,1)S(1)}, bf16[64,2048]{1,0:T(8,128)(2,1)S(1)}, u32[]{:S(2)}, u32[]{:S(2)}) %collective-permute-start.17) | collective-permute-done | bytes 262176 | tf_op jit(solution)/shard_map/ppermute | solution.py:219
  61.5 3.8 %collective-permute-start.18 = (bf16[64,2048]{1,0:T(8,128)(2,1)S(1)}, bf16[64,2048]{1,0:T(8,128)(2,1)S(1)}, u32[]{:S(2)}, u32[]{:S(2)}) collective-permute-start(bf16[64,2048]{1,0:T(8,128)(2,1)S(1)} %fusion.5), channel_id=1, source_target_pairs={{0,8},{1,9},{2,10},{3,11},{4,12},{5,13},{6,14},{7,15},{8,0},{9,1},... | collective-permute-start | bytes 786440 | tf_op jit(solution)/shard_map/ppermute | solution.py:219
  65.3 1.7 %collective-permute-done.24 = bf16[64,2048]{1,0:T(8,128)(2,1)S(1)} collective-permute-done((bf16[64,2048]{1,0:T(8,128)(2,1)S(1)}, bf16[64,2048]{1,0:T(8,128)(2,1)S(1)}, u32[]{:S(2)}, u32[]{:S(2)}) %collective-permute-start.24) | collective-permute-done | bytes 262176 | tf_op jit(solution)/shard_map/ppermute | solution.py:219
  67.1 1.3 %collective-permute-start.25 = (bf16[64,2048]{1,0:T(8,128)(2,1)S(1)}, bf16[64,2048]{1,0:T(8,128)(2,1)S(1)}, u32[]{:S(2)}, u32[]{:S(2)}) collective-permute-start(bf16[64,2048]{1,0:T(8,128)(2,1)S(1)} %fusion.2), channel_id=1, source_target_pairs={{0,12},{1,13},{2,14},{3,15},{4,8},{5,9},{6,10},{7,11},{8,4},{9,5},... | collective-permute-start | bytes 786440 | tf_op jit(solution)/shard_map/ppermute | solution.py:219
  68.3 12.8 %collective-permute-done.18 = bf16[64,2048]{1,0:T(8,128)(2,1)S(1)} collective-permute-done((bf16[64,2048]{1,0:T(8,128)(2,1)S(1)}, bf16[64,2048]{1,0:T(8,128)(2,1)S(1)}, u32[]{:S(2)}, u32[]{:S(2)}) %collective-permute-start.18) | collective-permute-done | bytes 262176 | tf_op jit(solution)/shard_map/ppermute | solution.py:219
  81.1 6.8 %collective-permute-done.25 = bf16[64,2048]{1,0:T(8,128)(2,1)S(1)} collective-permute-done((bf16[64,2048]{1,0:T(8,128)(2,1)S(1)}, bf16[64,2048]{1,0:T(8,128)(2,1)S(1)}, u32[]{:S(2)}, u32[]{:S(2)}) %collective-permute-start.25) | collective-permute-done | bytes 262176 | tf_op jit(solution)/shard_map/ppermute | solution.py:219
  87.9 0.9 %fusion.14 = bf16[64,2048]{1,0:T(8,128)(2,1)} fusion(f32[64,2048]{1,0:T(8,128)S(1)} %get-tuple-element.17, f32[128,2048]{1,0:T(8,128)S(1)} %convert_element_type.57, bf16[64,2048]{1,0:T(8,128)(2,1)S(1)} %collective-permute-done.25, bf16[64,2048]{1,0:T(8,128)(2,1)S(1)} %collective-permute-done.18, bf16[64,2048]{1,0:T(8,128)(2,1)S(1)} %collective-permute-done.11, ...), kind=kLoop, calls=%fused_computation.22 | loop fusion | flops 1310720 | bytes 2359296 | tf_op jit(solution)/shard_map/convert_element_type | solution.py:259
  (51 shorter events, 3.6 us)
Async XLA Ops:
  1.9 8.7 %collective-permute-start = (bf16[64,2176]{1,0:T(8,128)(2,1)}, bf16[64,2176]{1,0:T(8,128)(2,1)S(1)}, u32[]{:S(2)}, u32[]{:S(2)}) collective-permute-start(bf16[64,2176]{1,0:T(8,128)(2,1)} %shard_map.73.refs_1_), channel_id=1, source_target_pairs={{0,2},{1,3},{2,0},{3,1},{4,6},{5,7},{6,4},{7,5},{8,10},{9,11},{10,... | collective-permute-start | bytes 835592 | tf_op jit(solution)/shard_map/ppermute | solution.py:219
  3.5 12.2 %collective-permute-start.5 = (bf16[64,2176]{1,0:T(8,128)(2,1)}, bf16[64,2176]{1,0:T(8,128)(2,1)S(1)}, u32[]{:S(2)}, u32[]{:S(2)}) collective-permute-start(bf16[64,2176]{1,0:T(8,128)(2,1)} %shard_map.73.refs_1_), channel_id=1, source_target_pairs={{0,4},{1,5},{2,6},{3,7},{4,0},{5,1},{6,2},{7,3},{8,12},{9,13},{10,... | collective-permute-start | bytes 835592 | tf_op jit(solution)/shard_map/ppermute | solution.py:219
  4.0 15.0 %collective-permute-start.12 = (bf16[64,2176]{1,0:T(8,128)(2,1)}, bf16[64,2176]{1,0:T(8,128)(2,1)S(1)}, u32[]{:S(2)}, u32[]{:S(2)}) collective-permute-start(bf16[64,2176]{1,0:T(8,128)(2,1)} %shard_map.73.refs_1_), channel_id=1, source_target_pairs={{0,8},{1,9},{2,10},{3,11},{4,12},{5,13},{6,14},{7,15},{8,0},{9,1},... | collective-permute-start | bytes 835592 | tf_op jit(solution)/shard_map/ppermute | solution.py:219
  6.5 12.9 %collective-permute-start.1 = (bf16[64,2176]{1,0:T(8,128)(2,1)}, bf16[64,2176]{1,0:T(8,128)(2,1)S(1)}, u32[]{:S(2)}, u32[]{:S(2)}) collective-permute-start(bf16[64,2176]{1,0:T(8,128)(2,1)} %shard_map.73.refs_1_), channel_id=1, source_target_pairs={{0,1},{1,0},{2,3},{3,2},{4,5},{5,4},{6,7},{7,6},{8,9},{9,8},{10,11... | collective-permute-start | bytes 835592 | tf_op jit(solution)/shard_map/ppermute | solution.py:219
  10.6 11.4 %collective-permute-start.2 = (bf16[64,2176]{1,0:T(8,128)(2,1)S(1)}, bf16[64,2176]{1,0:T(8,128)(2,1)S(1)}, u32[]{:S(2)}, u32[]{:S(2)}) collective-permute-start(bf16[64,2176]{1,0:T(8,128)(2,1)S(1)} %collective-permute-done.refs_2_), channel_id=1, source_target_pairs={{0,1},{1,0},{2,3},{3,2},{4,5},{5,4},{6,7},{7,6},{8,9},{9,8},{10,11... | collective-permute-start | bytes 835592 | tf_op jit(solution)/shard_map/ppermute | solution.py:219
  15.7 15.7 %collective-permute-start.6 = (bf16[64,2176]{1,0:T(8,128)(2,1)S(1)}, bf16[64,2176]{1,0:T(8,128)(2,1)S(1)}, u32[]{:S(2)}, u32[]{:S(2)}) collective-permute-start(bf16[64,2176]{1,0:T(8,128)(2,1)S(1)} %collective-permute-done.5.refs_1_), channel_id=1, source_target_pairs={{0,2},{1,3},{2,0},{3,1},{4,6},{5,7},{6,4},{7,5},{8,10},{9,11},{10,... | collective-permute-start | bytes 835592 | tf_op jit(solution)/shard_map/ppermute | solution.py:219
  16.3 15.7 %collective-permute-start.7 = (bf16[64,2176]{1,0:T(8,128)(2,1)S(1)}, bf16[64,2176]{1,0:T(8,128)(2,1)S(1)}, u32[]{:S(2)}, u32[]{:S(2)}) collective-permute-start(bf16[64,2176]{1,0:T(8,128)(2,1)S(1)} %collective-permute-done.5.refs_1_), channel_id=1, source_target_pairs={{0,1},{1,0},{2,3},{3,2},{4,5},{5,4},{6,7},{7,6},{8,9},{9,8},{10,11... | collective-permute-start | bytes 835592 | tf_op jit(solution)/shard_map/ppermute | solution.py:219
  18.9 13.1 %collective-permute-start.13 = (bf16[64,2176]{1,0:T(8,128)(2,1)S(1)}, bf16[64,2176]{1,0:T(8,128)(2,1)S(1)}, u32[]{:S(2)}, u32[]{:S(2)}) collective-permute-start(bf16[64,2176]{1,0:T(8,128)(2,1)S(1)} %collective-permute-done.12.refs_1_), channel_id=1, source_target_pairs={{0,2},{1,3},{2,0},{3,1},{4,6},{5,7},{6,4},{7,5},{8,10},{9,11},{10,... | collective-permute-start | bytes 835592 | tf_op jit(solution)/shard_map/ppermute | solution.py:219
  19.5 13.1 %collective-permute-start.19 = (bf16[64,2176]{1,0:T(8,128)(2,1)S(1)}, bf16[64,2176]{1,0:T(8,128)(2,1)S(1)}, u32[]{:S(2)}, u32[]{:S(2)}) collective-permute-start(bf16[64,2176]{1,0:T(8,128)(2,1)S(1)} %collective-permute-done.5.refs_1_), channel_id=1, source_target_pairs={{0,8},{1,9},{2,10},{3,11},{4,12},{5,13},{6,14},{7,15},{8,0},{9,1},... | collective-permute-start | bytes 835592 | tf_op jit(solution)/shard_map/ppermute | solution.py:219
  22.0 1.9 %copy-start = (bf16[1,2048,768]{2,1,0:T(8,128)(2,1)S(1)}, bf16[1,2048,768]{2,1,0:T(8,128)(2,1)}, u32[]{:S(2)}) copy-start(bf16[1,2048,768]{2,1,0:T(8,128)(2,1)} %refs_5_.7) | copy-start | bytes 9437188
  23.9 1.9 %copy-start.2 = (bf16[1,2048,768]{2,1,0:T(8,128)(2,1)S(1)}, bf16[1,2048,768]{2,1,0:T(8,128)(2,1)}, u32[]{:S(2)}) copy-start(bf16[1,2048,768]{2,1,0:T(8,128)(2,1)} %refs_6_.7) | copy-start | bytes 9437188
  25.8 1.9 %copy-start.4 = (bf16[1,768,2048]{2,1,0:T(8,128)(2,1)S(1)}, bf16[1,768,2048]{2,1,0:T(8,128)(2,1)}, u32[]{:S(2)}) copy-start(bf16[1,768,2048]{2,1,0:T(8,128)(2,1)} %refs_7_.7) | copy-start | bytes 9437188
  28.7 5.3 %copy-start.1 = (bf16[1,2048,768]{2,1,0:T(8,128)(2,1)S(1)}, bf16[1,2048,768]{2,1,0:T(8,128)(2,1)}, u32[]{:S(2)}) copy-start(bf16[1,2048,768]{2,1,0:T(8,128)(2,1)} %refs_5_.7) | copy-start | bytes 9437188
  28.7 5.3 %copy-start.3 = (bf16[1,2048,768]{2,1,0:T(8,128)(2,1)S(1)}, bf16[1,2048,768]{2,1,0:T(8,128)(2,1)}, u32[]{:S(2)}) copy-start(bf16[1,2048,768]{2,1,0:T(8,128)(2,1)} %refs_6_.7) | copy-start | bytes 9437188
  28.7 5.3 %copy-start.5 = (bf16[1,768,2048]{2,1,0:T(8,128)(2,1)S(1)}, bf16[1,768,2048]{2,1,0:T(8,128)(2,1)}, u32[]{:S(2)}) copy-start(bf16[1,768,2048]{2,1,0:T(8,128)(2,1)} %refs_7_.7) | copy-start | bytes 9437188
  31.4 9.8 %collective-permute-start.3 = (bf16[128,2048]{1,0:T(8,128)(2,1)S(1)}, bf16[128,2048]{1,0:T(8,128)(2,1)S(1)}, u32[]{:S(2)}, u32[]{:S(2)}) collective-permute-start(bf16[128,2048]{1,0:T(8,128)(2,1)S(1)} %get-tuple-element.18), channel_id=1, source_target_pairs={{0,1},{1,0},{2,3},{3,2},{4,5},{5,4},{6,7},{7,6},{8,9},{9,8},{10,11... | collective-permute-start | bytes 1572872 | tf_op jit(solution)/shard_map/ppermute | solution.py:219
  31.5 2.5 %collective-permute-start.8 = (bf16[64,2176]{1,0:T(8,128)(2,1)S(1)}, bf16[64,2176]{1,0:T(8,128)(2,1)S(1)}, u32[]{:S(2)}, u32[]{:S(2)}) collective-permute-start(bf16[64,2176]{1,0:T(8,128)(2,1)S(1)} %collective-permute-done.6.refs_2_), channel_id=1, source_target_pairs={{0,1},{1,0},{2,3},{3,2},{4,5},{5,4},{6,7},{7,6},{8,9},{9,8},{10,11... | collective-permute-start | bytes 835592 | tf_op jit(solution)/shard_map/ppermute | solution.py:219
  31.9 4.8 %collective-permute-start.14 = (bf16[64,2176]{1,0:T(8,128)(2,1)S(1)}, bf16[64,2176]{1,0:T(8,128)(2,1)S(1)}, u32[]{:S(2)}, u32[]{:S(2)}) collective-permute-start(bf16[64,2176]{1,0:T(8,128)(2,1)S(1)} %collective-permute-done.12.refs_1_), channel_id=1, source_target_pairs={{0,1},{1,0},{2,3},{3,2},{4,5},{5,4},{6,7},{7,6},{8,9},{9,8},{10,11... | collective-permute-start | bytes 835592 | tf_op jit(solution)/shard_map/ppermute | solution.py:219
  32.0 5.2 %collective-permute-start.15 = (bf16[64,2176]{1,0:T(8,128)(2,1)S(1)}, bf16[64,2176]{1,0:T(8,128)(2,1)S(1)}, u32[]{:S(2)}, u32[]{:S(2)}) collective-permute-start(bf16[64,2176]{1,0:T(8,128)(2,1)S(1)} %collective-permute-done.13.refs_2_), channel_id=1, source_target_pairs={{0,1},{1,0},{2,3},{3,2},{4,5},{5,4},{6,7},{7,6},{8,9},{9,8},{10,11... | collective-permute-start | bytes 835592 | tf_op jit(solution)/shard_map/ppermute | solution.py:219
  32.6 8.6 %collective-permute-start.20 = (bf16[64,2176]{1,0:T(8,128)(2,1)S(1)}, bf16[64,2176]{1,0:T(8,128)(2,1)S(1)}, u32[]{:S(2)}, u32[]{:S(2)}) collective-permute-start(bf16[64,2176]{1,0:T(8,128)(2,1)S(1)} %collective-permute-done.19.refs_1_), channel_id=1, source_target_pairs={{0,2},{1,3},{2,0},{3,1},{4,6},{5,7},{6,4},{7,5},{8,10},{9,11},{10,... | collective-permute-start | bytes 835592 | tf_op jit(solution)/shard_map/ppermute | solution.py:219
  36.7 9.2 %collective-permute-start.9 = (bf16[128,2048]{1,0:T(8,128)(2,1)S(1)}, bf16[128,2048]{1,0:T(8,128)(2,1)S(1)}, u32[]{:S(2)}, u32[]{:S(2)}) collective-permute-start(bf16[128,2048]{1,0:T(8,128)(2,1)S(1)} %get-tuple-element.21), channel_id=1, source_target_pairs={{0,1},{1,0},{2,3},{3,2},{4,5},{5,4},{6,7},{7,6},{8,9},{9,8},{10,11... | collective-permute-start | bytes 1572872 | tf_op jit(solution)/shard_map/ppermute | solution.py:219
  36.8 6.1 %collective-permute-start.21 = (bf16[64,2176]{1,0:T(8,128)(2,1)S(1)}, bf16[64,2176]{1,0:T(8,128)(2,1)S(1)}, u32[]{:S(2)}, u32[]{:S(2)}) collective-permute-start(bf16[64,2176]{1,0:T(8,128)(2,1)S(1)} %collective-permute-done.19.refs_1_), channel_id=1, source_target_pairs={{0,1},{1,0},{2,3},{3,2},{4,5},{5,4},{6,7},{7,6},{8,9},{9,8},{10,11... | collective-permute-start | bytes 835592 | tf_op jit(solution)/shard_map/ppermute | solution.py:219
  39.9 7.4 %collective-permute-start.16 = (bf16[128,2048]{1,0:T(8,128)(2,1)S(1)}, bf16[128,2048]{1,0:T(8,128)(2,1)S(1)}, u32[]{:S(2)}, u32[]{:S(2)}) collective-permute-start(bf16[128,2048]{1,0:T(8,128)(2,1)S(1)} %get-tuple-element.24), channel_id=1, source_target_pairs={{0,1},{1,0},{2,3},{3,2},{4,5},{5,4},{6,7},{7,6},{8,9},{9,8},{10,11... | collective-permute-start | bytes 1572872 | tf_op jit(solution)/shard_map/ppermute | solution.py:219
  41.1 1.7 %collective-permute-start.22 = (bf16[64,2176]{1,0:T(8,128)(2,1)S(1)}, bf16[64,2176]{1,0:T(8,128)(2,1)S(1)}, u32[]{:S(2)}, u32[]{:S(2)}) collective-permute-start(bf16[64,2176]{1,0:T(8,128)(2,1)S(1)} %collective-permute-done.20.refs_2_), channel_id=1, source_target_pairs={{0,1},{1,0},{2,3},{3,2},{4,5},{5,4},{6,7},{7,6},{8,9},{9,8},{10,11... | collective-permute-start | bytes 835592 | tf_op jit(solution)/shard_map/ppermute | solution.py:219
  41.3 27.0 %collective-permute-start.4 = (bf16[64,2048]{1,0:T(8,128)(2,1)S(1)}, bf16[64,2048]{1,0:T(8,128)(2,1)S(1)}, u32[]{:S(2)}, u32[]{:S(2)}) collective-permute-start(bf16[64,2048]{1,0:T(8,128)(2,1)S(1)} %fusion.9), channel_id=1, source_target_pairs={{0,2},{1,3},{2,0},{3,1},{4,6},{5,7},{6,4},{7,5},{8,10},{9,11},{10,... | collective-permute-start | bytes 786440 | tf_op jit(solution)/shard_map/ppermute | solution.py:219
  45.5 13.8 %collective-permute-start.23 = (bf16[128,2048]{1,0:T(8,128)(2,1)S(1)}, bf16[128,2048]{1,0:T(8,128)(2,1)S(1)}, u32[]{:S(2)}, u32[]{:S(2)}) collective-permute-start(bf16[128,2048]{1,0:T(8,128)(2,1)S(1)} %get-tuple-element.27), channel_id=1, source_target_pairs={{0,1},{1,0},{2,3},{3,2},{4,5},{5,4},{6,7},{7,6},{8,9},{9,8},{10,11... | collective-permute-start | bytes 1572872 | tf_op jit(solution)/shard_map/ppermute | solution.py:219
  46.0 10.1 %collective-permute-start.10 = (bf16[64,2048]{1,0:T(8,128)(2,1)S(1)}, bf16[64,2048]{1,0:T(8,128)(2,1)S(1)}, u32[]{:S(2)}, u32[]{:S(2)}) collective-permute-start(bf16[64,2048]{1,0:T(8,128)(2,1)S(1)} %fusion.6), channel_id=1, source_target_pairs={{0,2},{1,3},{2,0},{3,1},{4,6},{5,7},{6,4},{7,5},{8,10},{9,11},{10,... | collective-permute-start | bytes 786440 | tf_op jit(solution)/shard_map/ppermute | solution.py:219
  47.5 13.9 %collective-permute-start.17 = (bf16[64,2048]{1,0:T(8,128)(2,1)S(1)}, bf16[64,2048]{1,0:T(8,128)(2,1)S(1)}, u32[]{:S(2)}, u32[]{:S(2)}) collective-permute-start(bf16[64,2048]{1,0:T(8,128)(2,1)S(1)} %fusion.3), channel_id=1, source_target_pairs={{0,2},{1,3},{2,0},{3,1},{4,6},{5,7},{6,4},{7,5},{8,10},{9,11},{10,... | collective-permute-start | bytes 786440 | tf_op jit(solution)/shard_map/ppermute | solution.py:219
  56.2 12.1 %collective-permute-start.11 = (bf16[64,2048]{1,0:T(8,128)(2,1)S(1)}, bf16[64,2048]{1,0:T(8,128)(2,1)S(1)}, u32[]{:S(2)}, u32[]{:S(2)}) collective-permute-start(bf16[64,2048]{1,0:T(8,128)(2,1)S(1)} %fusion.8), channel_id=1, source_target_pairs={{0,4},{1,5},{2,6},{3,7},{4,0},{5,1},{6,2},{7,3},{8,12},{9,13},{10,... | collective-permute-start | bytes 786440 | tf_op jit(solution)/shard_map/ppermute | solution.py:219
  59.5 7.4 %collective-permute-start.24 = (bf16[64,2048]{1,0:T(8,128)(2,1)S(1)}, bf16[64,2048]{1,0:T(8,128)(2,1)S(1)}, u32[]{:S(2)}, u32[]{:S(2)}) collective-permute-start(bf16[64,2048]{1,0:T(8,128)(2,1)S(1)} %fusion), channel_id=1, source_target_pairs={{0,2},{1,3},{2,0},{3,1},{4,6},{5,7},{6,4},{7,5},{8,10},{9,11},{10,... | collective-permute-start | bytes 786440 | tf_op jit(solution)/shard_map/ppermute | solution.py:219
  61.5 19.7 %collective-permute-start.18 = (bf16[64,2048]{1,0:T(8,128)(2,1)S(1)}, bf16[64,2048]{1,0:T(8,128)(2,1)S(1)}, u32[]{:S(2)}, u32[]{:S(2)}) collective-permute-start(bf16[64,2048]{1,0:T(8,128)(2,1)S(1)} %fusion.5), channel_id=1, source_target_pairs={{0,8},{1,9},{2,10},{3,11},{4,12},{5,13},{6,14},{7,15},{8,0},{9,1},... | collective-permute-start | bytes 786440 | tf_op jit(solution)/shard_map/ppermute | solution.py:219
  67.1 20.9 %collective-permute-start.25 = (bf16[64,2048]{1,0:T(8,128)(2,1)S(1)}, bf16[64,2048]{1,0:T(8,128)(2,1)S(1)}, u32[]{:S(2)}, u32[]{:S(2)}) collective-permute-start(bf16[64,2048]{1,0:T(8,128)(2,1)S(1)} %fusion.2), channel_id=1, source_target_pairs={{0,12},{1,13},{2,14},{3,15},{4,8},{5,9},{6,10},{7,11},{8,4},{9,5},... | collective-permute-start | bytes 786440 | tf_op jit(solution)/shard_map/ppermute | solution.py:219
  (1 other events, 1.0 us)

commit v3 on v2

--- a/solution.py
+++ b/solution.py
@@ -9,6 +9,8 @@
 
 LANES = 128
 CHUNK = 256
+FIRST = 'K0'
+FIRST_LIMIT = 41 * 2**20
 STEPS = [
     ('A4', []),
     ('A8', []),
@@ -26,20 +28,20 @@
     ('A13', []),
     ('A15', []),
     ('K0', []),
-    ('O0', []),
-    ('X0', []),
-    ('K4', []),
-    ('O4', []),
-    ('X4', []),
-    ('K8', []),
+    ('K8', ['K0']),
     ('O8', []),
     ('X8', []),
-    ('K12', []),
+    ('K4', ['K0']),
+    ('O0', []),
+    ('O4', []),
+    ('X4', ['X8']),
+    ('K12', ['O8']),
     ('O12', []),
     ('X12', []),
-    ('Z4', []),
+    ('X0', ['X12']),
     ('Z8', []),
     ('Z12', []),
+    ('Z4', []),
 ]
 VMEM_LIMIT = 24 * 2**20
 
@@ -192,22 +194,43 @@
     experts_on(expert_total, me_ref, blocks, outs, *weights, hidden_ref)
 
 
-def weighted_outputs(expert_total, me, blocks, weights):
+def first_kernel(expert_total, number, *refs):
+    me_ref, blocks, sources, rest = refs[0], refs[1 : 1 + number], refs[1 + number : 4 + number], refs[4 + number :]
+    outs, weights, hidden_ref, sems = rest[:3], rest[3:6], rest[6], rest[7]
+    copies = []
+    for index, (source, target) in enumerate(zip(sources, weights, strict=True)):
+        half = source.shape[1] // 2
+        for part in range(2):
+            lines = slice(part * half, (part + 1) * half)
+            copies.append(
+                pltpu.make_async_copy(source.at[:, lines, :], target.at[:, lines, :], sems.at[2 * index + part])
+            )
+            copies[-1].start()
+    for copy in copies:
+        copy.wait()
+    experts_on(expert_total, me_ref, blocks, outs, *weights, hidden_ref)
+
+
+def weighted_outputs(expert_total, me, blocks, weights, first):
     count = blocks[0].shape[0]
     rows = sum(block.shape[0] for block in blocks)
     hidden_width, width = weights[2].shape[1:]
     vmem = pl.BlockSpec(memory_space=pltpu.VMEM)
     return pl.pallas_call(
-        functools.partial(expert_kernel, expert_total, len(blocks)),
-        in_specs=[pl.BlockSpec(memory_space=pltpu.SMEM)] + [vmem] * (len(blocks) + 3),
-        out_specs=[vmem] * 3,
+        functools.partial(first_kernel if first else expert_kernel, expert_total, len(blocks)),
+        in_specs=[pl.BlockSpec(memory_space=pltpu.SMEM)]
+        + [vmem] * len(blocks)
+        + [pl.BlockSpec(memory_space=pl.ANY) if first else vmem] * 3,
+        out_specs=[vmem] * (6 if first else 3),
         out_shape=[
             jax.ShapeDtypeStruct((count, width), jnp.float32),
             jax.ShapeDtypeStruct((count, width), jnp.float32),
             jax.ShapeDtypeStruct((rows - 2 * count, width), jnp.bfloat16),
-        ],
-        scratch_shapes=[pltpu.VMEM((rows, hidden_width), jnp.bfloat16)],
-        compiler_params=pltpu.CompilerParams(vmem_limit_bytes=VMEM_LIMIT),
+        ]
+        + [jax.ShapeDtypeStruct(array.shape, array.dtype) for array in weights if first],
+        scratch_shapes=[pltpu.VMEM((rows, hidden_width), jnp.bfloat16)]
+        + [pltpu.SemaphoreType.DMA((6,))] * first,
+        compiler_params=pltpu.CompilerParams(vmem_limit_bytes=FIRST_LIMIT if first else VMEM_LIMIT),
         cost_estimate=pl.CostEstimate(flops=1, bytes_accessed=1, transcendentals=0),
     )(me, *blocks, *weights)
 
@@ -228,8 +251,12 @@
     done = {"A0": pack_rows(tokens, scales, expert_ids, gate_weights, peer_count)}
     own, other, sums = {}, {}, {}
     for step, ties in STEPS:
-        kind, number = step[0], int(step[1:])
-        if kind == "A":
+        kind, number = step[0], int(step[1:] or 0)
+        if kind == "W":
+            one = after(jnp.ones((), jnp.bfloat16), ["A0"] + ties)
+            weights = tuple(array * one for array in weights)
+            done[step] = weights[-1]
+        elif kind == "A":
             bit = number & -number if number % 4 else 1 << (number.bit_length() - 1)
             done[step] = exchange(after(done["A%d" % (number - bit)], ties), bit)
         elif kind == "B":
@@ -240,7 +267,8 @@
             names += ["B%d" % number] if "B%d" % number in done else ["A%d" % (number + 1), "A%d" % (number + 3)]
             blocks = [done[name] for name in names]
             blocks[0] = after(blocks[0], ties)
-            parts = weighted_outputs(peer_count, me, blocks, weights)
+            parts = weighted_outputs(peer_count, me, blocks, weights, step == FIRST)
+            weights = parts[3:] or weights
             done[step] = parts[0]
             own[number], other[number] = parts[:2], parts[2]
         elif kind == "O":

time: 89.3 us -> 80.6 us (0.903)
  local copies, waits for them, and re-layouts: 6.63 us -> 0.95 us
  starting transfers between devices: 24.3 us -> 19.6 us
  Pallas kernels: 12.7 us -> 16.4 us
  waiting for transfers between devices: 43.3 us -> 41.5 us
    unnamed x14 -> x2, local copies, waits for them, and re-layouts: 6.63 us -> 0.95 us
    ppermute x26, starting transfers between devices: 24.3 us -> 19.6 us  [exchange(): lax.ppermute(array, 'expert', [(i, i ^ mask) for i in range(peer_count)])]
    pallas_call x4, Pallas kernels: 10.7 us -> 14.5 us  [weighted_outputs(): pl.pallas_call(functools.partial(first_kernel if first else expert_kernel...]
    ppermute x26, waiting for transfers between devices: 43.3 us -> 41.5 us  [exchange(): lax.ppermute(array, 'expert', [(i, i ^ mask) for i in range(peer_count)])]
  transfers between devices with their start and end apart: 26 -> 26, of which waited for: 10 -> 12; matrix products, arithmetic and copies ran while one was open for 1% -> 1% of each run, Pallas kernels for 12% -> 18%
where the time goes in v3:
time: 80.6 us; the launch traced here: 80.4 us
  waiting for transfers between devices  41.5 us (51%)
  starting transfers between devices  19.6 us (24%)
  Pallas kernels  16.4 us (20%)
  other arithmetic  1.79 us (2%)
  local copies, waits for them, and re-layouts  0.95 us (1%)
    ppermute x26, waiting for transfers between devices, exchange(): lax.ppermute(array, 'expert', [(i, i ^ mask) for i in range(peer_count)])  41.5 us
    ppermute x26, starting transfers between devices, exchange(): lax.ppermute(array, 'expert', [(i, i ^ mask) for i in range(peer_count)])  19.6 us
    pallas_call x4, Pallas kernels, weighted_outputs(): pl.pallas_call(functools.partial(first_kernel if first else expert_kernel...  14.5 us
    pallas_call x1, Pallas kernels, pack_rows(): pl.pallas_call(functools.partial(pack_kernel, expert_total), in_specs=[pl...  1.94 us
  transfers between devices with their start and end apart: 26, of which 12 were waited for; matrix products, arithmetic and copies ran while one was open for 1% of the time, Pallas kernels for 18%

profile of v3, /device:TPU:12, one launch (start us, length us, event | category | flops | bytes accessed | tf_op | source)
XLA Modules:
  0.0 80.4 jit_solution(6839268961539517334)
XLA Ops:
  0.0 1.9 %shard_map.73.refs_1_ = bf16[64,2176]{1,0:T(8,128)(2,1)} custom-call(bf16[64,2048]{1,0:T(8,128)(2,1)} %refs_0_.1, bf16[16,64]{1,0:T(8,128)(2,1)} %bitcast.4, s32[8,64]{1,0:T(8,128)} %bitcast.5, f32[8,64]{1,0:T(8,128)} %bitcast.6), custom_call_target="tpu_custom_call" | custom-call | flops 1 | bytes 1 | tf_op jit(solution)/shard_map/pallas_call | solution.py:154
  1.9 1.6 %collective-permute-start = (bf16[64,2176]{1,0:T(8,128)(2,1)}, bf16[64,2176]{1,0:T(8,128)(2,1)S(1)}, u32[]{:S(2)}, u32[]{:S(2)}) collective-permute-start(bf16[64,2176]{1,0:T(8,128)(2,1)} %shard_map.73.refs_1_), channel_id=1, source_target_pairs={{0,2},{1,3},{2,0},{3,1},{4,6},{5,7},{6,4},{7,5},{8,10},{9,11},{10,... | collective-permute-start | bytes 835592 | tf_op jit(solution)/shard_map/ppermute | solution.py:242
  3.5 2.6 %collective-permute-start.6 = (bf16[64,2176]{1,0:T(8,128)(2,1)}, bf16[64,2176]{1,0:T(8,128)(2,1)S(1)}, u32[]{:S(2)}, u32[]{:S(2)}) collective-permute-start(bf16[64,2176]{1,0:T(8,128)(2,1)} %shard_map.73.refs_1_), channel_id=1, source_target_pairs={{0,8},{1,9},{2,10},{3,11},{4,12},{5,13},{6,14},{7,15},{8,0},{9,1},... | collective-permute-start | bytes 835592 | tf_op jit(solution)/shard_map/ppermute | solution.py:242
  6.1 0.4 collective-permute-start.4
  6.5 4.1 %collective-permute-done.refs_2_ = bf16[64,2176]{1,0:T(8,128)(2,1)S(1)} collective-permute-done((bf16[64,2176]{1,0:T(8,128)(2,1)}, bf16[64,2176]{1,0:T(8,128)(2,1)S(1)}, u32[]{:S(2)}, u32[]{:S(2)}) %collective-permute-start) | collective-permute-done | bytes 278560 | tf_op jit(solution)/shard_map/ppermute | solution.py:242
  10.6 7.3 %collective-permute-done.6.refs_1_ = bf16[64,2176]{1,0:T(8,128)(2,1)S(1)} collective-permute-done((bf16[64,2176]{1,0:T(8,128)(2,1)}, bf16[64,2176]{1,0:T(8,128)(2,1)S(1)}, u32[]{:S(2)}, u32[]{:S(2)}) %collective-permute-start.6) | collective-permute-done | bytes 278560 | tf_op jit(solution)/shard_map/ppermute | solution.py:242
  17.9 0.5 collective-permute-start.7
  18.9 2.9 %collective-permute-start.5 = (bf16[64,2176]{1,0:T(8,128)(2,1)S(1)}, bf16[64,2176]{1,0:T(8,128)(2,1)S(1)}, u32[]{:S(2)}, u32[]{:S(2)}) collective-permute-start(bf16[64,2176]{1,0:T(8,128)(2,1)S(1)} %collective-permute-done.4.refs_1_), channel_id=1, source_target_pairs={{0,8},{1,9},{2,10},{3,11},{4,12},{5,13},{6,14},{7,15},{8,0},{9,1},... | collective-permute-start | bytes 835592 | tf_op jit(solution)/shard_map/ppermute | solution.py:242
  21.7 1.5 %collective-permute-start.17 = (bf16[64,2176]{1,0:T(8,128)(2,1)S(1)}, bf16[64,2176]{1,0:T(8,128)(2,1)S(1)}, u32[]{:S(2)}, u32[]{:S(2)}) collective-permute-start(bf16[64,2176]{1,0:T(8,128)(2,1)S(1)} %collective-permute-done.4.refs_1_), channel_id=1, source_target_pairs={{0,2},{1,3},{2,0},{3,1},{4,6},{5,7},{6,4},{7,5},{8,10},{9,11},{10,... | collective-permute-start | bytes 835592 | tf_op jit(solution)/shard_map/ppermute | solution.py:242
  23.2 0.9 %copy-done = bf16[64,2176]{1,0:T(8,128)(2,1)S(1)} copy-done((bf16[64,2176]{1,0:T(8,128)(2,1)S(1)}, bf16[64,2176]{1,0:T(8,128)(2,1)}, u32[]{:S(2)}) %copy-start) | copy-done | bytes 278552
  24.2 6.5 %shard_map.74 = (f32[64,2048]{1,0:T(8,128)S(1)}, f32[64,2048]{1,0:T(8,128)S(1)}, bf16[128,2048]{1,0:T(8,128)(2,1)S(1)}, bf16[1,2048,768]{2,1,0:T(8,128)(2,1)S(1)...) custom-call(s32[1]{0:T(128)} %bitcast.refs_0_, bf16[64,2176]{1,0:T(8,128)(2,1)S(1)} %copy-done, ...), custom_call_target="tpu_custom_call" | custom-call | flops 1 | bytes 1 | tf_op jit(solution)/shard_map/pallas_call | solution.py:219
  30.6 0.6 collective-permute-start.3
  31.7 0.7 collective-permute-done.17.refs_2_
  32.5 0.5 collective-permute-start.11
  33.2 2.7 %shard_map.75 = (f32[64,2048]{1,0:T(8,128)S(1)}, f32[64,2048]{1,0:T(8,128)S(1)}, bf16[128,2048]{1,0:T(8,128)(2,1)S(1)}) custom-call(s32[1]{0:T(128)} %bitcast.refs_0_, bf16[64,2176]{1,0:T(8,128)(2,1)S(1)} %collective-permute-done.6.refs_1_, bf16[64,2176]{1,0:T(8,128)(2,1)S(1)} %collective-permute-done.7.refs_2_, ...), custom_call_target="tpu_custom_call" | custom-call | flops 1 | bytes 1 | tf_op jit(solution)/shard_map/pallas_call | solution.py:219
  35.8 0.4 collective-permute-start.10
  36.4 2.7 %shard_map.77 = (f32[64,2048]{1,0:T(8,128)S(1)}, f32[64,2048]{1,0:T(8,128)S(1)}, bf16[128,2048]{1,0:T(8,128)(2,1)S(1)}) custom-call(s32[1]{0:T(128)} %bitcast.refs_0_, bf16[64,2176]{1,0:T(8,128)(2,1)S(1)} %collective-permute-done.4.refs_1_, bf16[64,2176]{1,0:T(8,128)(2,1)S(1)} %collective-permute-done.17.refs_2_, ...), custom_call_target="tpu_custom_call" | custom-call | flops 1 | bytes 1 | tf_op jit(solution)/shard_map/pallas_call | solution.py:219
  39.1 0.4 collective-permute-start.20
  39.5 2.0 %collective-permute-done.11.refs_2_ = bf16[64,2176]{1,0:T(8,128)(2,1)S(1)} collective-permute-done((bf16[64,2176]{1,0:T(8,128)(2,1)S(1)}, bf16[64,2176]{1,0:T(8,128)(2,1)S(1)}, u32[]{:S(2)}, u32[]{:S(2)}) %collective-permute-start.11) | collective-permute-done | bytes 278560 | tf_op jit(solution)/shard_map/ppermute | solution.py:242
  41.9 0.6 collective-permute-start.21
  42.5 0.6 collective-permute-done.13.refs_4_
  43.1 2.7 %shard_map.76 = (f32[64,2048]{1,0:T(8,128)S(1)}, f32[64,2048]{1,0:T(8,128)S(1)}, bf16[128,2048]{1,0:T(8,128)(2,1)S(1)}) custom-call(s32[1]{0:T(128)} %bitcast.refs_0_, bf16[64,2176]{1,0:T(8,128)(2,1)S(1)} %collective-permute-done.5.refs_1_, bf16[64,2176]{1,0:T(8,128)(2,1)S(1)} %collective-permute-done.11.refs_2_, ...), custom_call_target="tpu_custom_call" | custom-call | flops 1 | bytes 1 | tf_op jit(solution)/shard_map/pallas_call | solution.py:219
  46.1 4.5 %collective-permute-done.21 = bf16[64,2048]{1,0:T(8,128)(2,1)S(1)} collective-permute-done((bf16[64,2048]{1,0:T(8,128)(2,1)S(1)}, bf16[64,2048]{1,0:T(8,128)(2,1)S(1)}, u32[]{:S(2)}, u32[]{:S(2)}) %collective-permute-start.21) | collective-permute-done | bytes 262176 | tf_op jit(solution)/shard_map/ppermute | solution.py:242
  50.8 3.3 %collective-permute-start.24 = (bf16[64,2048]{1,0:T(8,128)(2,1)S(1)}, bf16[64,2048]{1,0:T(8,128)(2,1)S(1)}, u32[]{:S(2)}, u32[]{:S(2)}) collective-permute-start(bf16[64,2048]{1,0:T(8,128)(2,1)S(1)} %fusion.3), channel_id=1, source_target_pairs={{0,8},{1,9},{2,10},{3,11},{4,12},{5,13},{6,14},{7,15},{8,0},{9,1},... | collective-permute-start | bytes 786440 | tf_op jit(solution)/shard_map/ppermute | solution.py:242
  54.1 0.5 collective-permute-start.22
  54.8 1.6 %collective-permute-start.15 = (bf16[64,2048]{1,0:T(8,128)(2,1)S(1)}, bf16[64,2048]{1,0:T(8,128)(2,1)S(1)}, u32[]{:S(2)}, u32[]{:S(2)}) collective-permute-start(bf16[64,2048]{1,0:T(8,128)(2,1)S(1)} %fusion.7), channel_id=1, source_target_pairs={{0,2},{1,3},{2,0},{3,1},{4,6},{5,7},{6,4},{7,5},{8,10},{9,11},{10,... | collective-permute-start | bytes 786440 | tf_op jit(solution)/shard_map/ppermute | solution.py:242
  56.4 7.0 %collective-permute-done.22 = bf16[64,2048]{1,0:T(8,128)(2,1)S(1)} collective-permute-done((bf16[64,2048]{1,0:T(8,128)(2,1)S(1)}, bf16[64,2048]{1,0:T(8,128)(2,1)S(1)}, u32[]{:S(2)}, u32[]{:S(2)}) %collective-permute-start.22) | collective-permute-done | bytes 262176 | tf_op jit(solution)/shard_map/ppermute | solution.py:242
  63.5 3.9 %collective-permute-done.15 = bf16[64,2048]{1,0:T(8,128)(2,1)S(1)} collective-permute-done((bf16[64,2048]{1,0:T(8,128)(2,1)S(1)}, bf16[64,2048]{1,0:T(8,128)(2,1)S(1)}, u32[]{:S(2)}, u32[]{:S(2)}) %collective-permute-start.15) | collective-permute-done | bytes 262176 | tf_op jit(solution)/shard_map/ppermute | solution.py:242
  67.5 1.1 %collective-permute-start.16 = (bf16[64,2048]{1,0:T(8,128)(2,1)S(1)}, bf16[64,2048]{1,0:T(8,128)(2,1)S(1)}, u32[]{:S(2)}, u32[]{:S(2)}) collective-permute-start(bf16[64,2048]{1,0:T(8,128)(2,1)S(1)} %fusion.9), channel_id=1, source_target_pairs={{0,2},{1,3},{2,0},{3,1},{4,6},{5,7},{6,4},{7,5},{8,10},{9,11},{10,... | collective-permute-start | bytes 786440 | tf_op jit(solution)/shard_map/ppermute | solution.py:242
  68.7 6.8 %collective-permute-done.23 = bf16[64,2048]{1,0:T(8,128)(2,1)S(1)} collective-permute-done((bf16[64,2048]{1,0:T(8,128)(2,1)S(1)}, bf16[64,2048]{1,0:T(8,128)(2,1)S(1)}, u32[]{:S(2)}, u32[]{:S(2)}) %collective-permute-start.23) | collective-permute-done | bytes 262176 | tf_op jit(solution)/shard_map/ppermute | solution.py:242
  75.5 4.0 %collective-permute-done.25 = bf16[64,2048]{1,0:T(8,128)(2,1)S(1)} collective-permute-done((bf16[64,2048]{1,0:T(8,128)(2,1)S(1)}, bf16[64,2048]{1,0:T(8,128)(2,1)S(1)}, u32[]{:S(2)}, u32[]{:S(2)}) %collective-permute-start.25) | collective-permute-done | bytes 262176 | tf_op jit(solution)/shard_map/ppermute | solution.py:242
  79.5 0.9 %fusion.14 = bf16[64,2048]{1,0:T(8,128)(2,1)} fusion(f32[64,2048]{1,0:T(8,128)S(1)} %get-tuple-element.25, f32[128,2048]{1,0:T(8,128)S(1)} %convert_element_type.57, bf16[64,2048]{1,0:T(8,128)(2,1)S(1)} %collective-permute-done.25, bf16[64,2048]{1,0:T(8,128)(2,1)S(1)} %collective-permute-done.24, bf16[64,2048]{1,0:T(8,128)(2,1)S(1)} %collective-permute-done.23, ...), kind=kLoop, calls=%fused_computation.22 | loop fusion | flops 1310720 | bytes 2359296 | tf_op jit(solution)/shard_map/convert_element_type | solution.py:287
  (39 shorter events, 2.5 us)
Async XLA Ops:
  1.9 8.7 %collective-permute-start = (bf16[64,2176]{1,0:T(8,128)(2,1)}, bf16[64,2176]{1,0:T(8,128)(2,1)S(1)}, u32[]{:S(2)}, u32[]{:S(2)}) collective-permute-start(bf16[64,2176]{1,0:T(8,128)(2,1)} %shard_map.73.refs_1_), channel_id=1, source_target_pairs={{0,2},{1,3},{2,0},{3,1},{4,6},{5,7},{6,4},{7,5},{8,10},{9,11},{10,... | collective-permute-start | bytes 835592 | tf_op jit(solution)/shard_map/ppermute | solution.py:242
  3.5 14.4 %collective-permute-start.6 = (bf16[64,2176]{1,0:T(8,128)(2,1)}, bf16[64,2176]{1,0:T(8,128)(2,1)S(1)}, u32[]{:S(2)}, u32[]{:S(2)}) collective-permute-start(bf16[64,2176]{1,0:T(8,128)(2,1)} %shard_map.73.refs_1_), channel_id=1, source_target_pairs={{0,8},{1,9},{2,10},{3,11},{4,12},{5,13},{6,14},{7,15},{8,0},{9,1},... | collective-permute-start | bytes 835592 | tf_op jit(solution)/shard_map/ppermute | solution.py:242
  6.1 12.8 %collective-permute-start.4 = (bf16[64,2176]{1,0:T(8,128)(2,1)}, bf16[64,2176]{1,0:T(8,128)(2,1)S(1)}, u32[]{:S(2)}, u32[]{:S(2)}) collective-permute-start(bf16[64,2176]{1,0:T(8,128)(2,1)} %shard_map.73.refs_1_), channel_id=1, source_target_pairs={{0,4},{1,5},{2,6},{3,7},{4,0},{5,1},{6,2},{7,3},{8,12},{9,13},{10,... | collective-permute-start | bytes 835592 | tf_op jit(solution)/shard_map/ppermute | solution.py:242
  6.5 16.7 %collective-permute-start.1 = (bf16[64,2176]{1,0:T(8,128)(2,1)}, bf16[64,2176]{1,0:T(8,128)(2,1)S(1)}, u32[]{:S(2)}, u32[]{:S(2)}) collective-permute-start(bf16[64,2176]{1,0:T(8,128)(2,1)} %shard_map.73.refs_1_), channel_id=1, source_target_pairs={{0,1},{1,0},{2,3},{3,2},{4,5},{5,4},{6,7},{7,6},{8,9},{9,8},{10,11... | collective-permute-start | bytes 835592 | tf_op jit(solution)/shard_map/ppermute | solution.py:242
  10.6 12.6 %collective-permute-start.2 = (bf16[64,2176]{1,0:T(8,128)(2,1)S(1)}, bf16[64,2176]{1,0:T(8,128)(2,1)S(1)}, u32[]{:S(2)}, u32[]{:S(2)}) collective-permute-start(bf16[64,2176]{1,0:T(8,128)(2,1)S(1)} %collective-permute-done.refs_2_), channel_id=1, source_target_pairs={{0,1},{1,0},{2,3},{3,2},{4,5},{5,4},{6,7},{7,6},{8,9},{9,8},{10,11... | collective-permute-start | bytes 835592 | tf_op jit(solution)/shard_map/ppermute | solution.py:242
  17.9 13.3 %collective-permute-start.7 = (bf16[64,2176]{1,0:T(8,128)(2,1)S(1)}, bf16[64,2176]{1,0:T(8,128)(2,1)S(1)}, u32[]{:S(2)}, u32[]{:S(2)}) collective-permute-start(bf16[64,2176]{1,0:T(8,128)(2,1)S(1)} %collective-permute-done.6.refs_1_), channel_id=1, source_target_pairs={{0,2},{1,3},{2,0},{3,1},{4,6},{5,7},{6,4},{7,5},{8,10},{9,11},{10,... | collective-permute-start | bytes 835592 | tf_op jit(solution)/shard_map/ppermute | solution.py:242
  18.9 12.5 %collective-permute-start.5 = (bf16[64,2176]{1,0:T(8,128)(2,1)S(1)}, bf16[64,2176]{1,0:T(8,128)(2,1)S(1)}, u32[]{:S(2)}, u32[]{:S(2)}) collective-permute-start(bf16[64,2176]{1,0:T(8,128)(2,1)S(1)} %collective-permute-done.4.refs_1_), channel_id=1, source_target_pairs={{0,8},{1,9},{2,10},{3,11},{4,12},{5,13},{6,14},{7,15},{8,0},{9,1},... | collective-permute-start | bytes 835592 | tf_op jit(solution)/shard_map/ppermute | solution.py:242
  21.7 10.7 %collective-permute-start.17 = (bf16[64,2176]{1,0:T(8,128)(2,1)S(1)}, bf16[64,2176]{1,0:T(8,128)(2,1)S(1)}, u32[]{:S(2)}, u32[]{:S(2)}) collective-permute-start(bf16[64,2176]{1,0:T(8,128)(2,1)S(1)} %collective-permute-done.4.refs_1_), channel_id=1, source_target_pairs={{0,2},{1,3},{2,0},{3,1},{4,6},{5,7},{6,4},{7,5},{8,10},{9,11},{10,... | collective-permute-start | bytes 835592 | tf_op jit(solution)/shard_map/ppermute | solution.py:242
  23.2 9.2 %collective-permute-start.8 = (bf16[64,2176]{1,0:T(8,128)(2,1)S(1)}, bf16[64,2176]{1,0:T(8,128)(2,1)S(1)}, u32[]{:S(2)}, u32[]{:S(2)}) collective-permute-start(bf16[64,2176]{1,0:T(8,128)(2,1)S(1)} %collective-permute-done.6.refs_1_), channel_id=1, source_target_pairs={{0,1},{1,0},{2,3},{3,2},{4,5},{5,4},{6,7},{7,6},{8,9},{9,8},{10,11... | collective-permute-start | bytes 835592 | tf_op jit(solution)/shard_map/ppermute | solution.py:242
  23.2 1.0 %copy-start = (bf16[64,2176]{1,0:T(8,128)(2,1)S(1)}, bf16[64,2176]{1,0:T(8,128)(2,1)}, u32[]{:S(2)}) copy-start(bf16[64,2176]{1,0:T(8,128)(2,1)} %shard_map.73.refs_1_) | copy-start | bytes 835588
  30.6 10.9 %collective-permute-start.3 = (bf16[128,2048]{1,0:T(8,128)(2,1)S(1)}, bf16[128,2048]{1,0:T(8,128)(2,1)S(1)}, u32[]{:S(2)}, u32[]{:S(2)}) collective-permute-start(bf16[128,2048]{1,0:T(8,128)(2,1)S(1)} %get-tuple-element.26), channel_id=1, source_target_pairs={{0,1},{1,0},{2,3},{3,2},{4,5},{5,4},{6,7},{7,6},{8,9},{9,8},{10,11... | collective-permute-start | bytes 1572872 | tf_op jit(solution)/shard_map/ppermute | solution.py:242
  31.2 1.9 %collective-permute-start.9 = (bf16[64,2176]{1,0:T(8,128)(2,1)S(1)}, bf16[64,2176]{1,0:T(8,128)(2,1)S(1)}, u32[]{:S(2)}, u32[]{:S(2)}) collective-permute-start(bf16[64,2176]{1,0:T(8,128)(2,1)S(1)} %collective-permute-done.7.refs_2_), channel_id=1, source_target_pairs={{0,1},{1,0},{2,3},{3,2},{4,5},{5,4},{6,7},{7,6},{8,9},{9,8},{10,11... | collective-permute-start | bytes 835592 | tf_op jit(solution)/shard_map/ppermute | solution.py:242
  31.3 5.0 %collective-permute-start.18 = (bf16[64,2176]{1,0:T(8,128)(2,1)S(1)}, bf16[64,2176]{1,0:T(8,128)(2,1)S(1)}, u32[]{:S(2)}, u32[]{:S(2)}) collective-permute-start(bf16[64,2176]{1,0:T(8,128)(2,1)S(1)} %collective-permute-done.4.refs_1_), channel_id=1, source_target_pairs={{0,1},{1,0},{2,3},{3,2},{4,5},{5,4},{6,7},{7,6},{8,9},{9,8},{10,11... | collective-permute-start | bytes 835592 | tf_op jit(solution)/shard_map/ppermute | solution.py:242
  32.4 4.0 %collective-permute-start.19 = (bf16[64,2176]{1,0:T(8,128)(2,1)S(1)}, bf16[64,2176]{1,0:T(8,128)(2,1)S(1)}, u32[]{:S(2)}, u32[]{:S(2)}) collective-permute-start(bf16[64,2176]{1,0:T(8,128)(2,1)S(1)} %collective-permute-done.17.refs_2_), channel_id=1, source_target_pairs={{0,1},{1,0},{2,3},{3,2},{4,5},{5,4},{6,7},{7,6},{8,9},{9,8},{10,11... | collective-permute-start | bytes 835592 | tf_op jit(solution)/shard_map/ppermute | solution.py:242
  32.5 9.1 %collective-permute-start.11 = (bf16[64,2176]{1,0:T(8,128)(2,1)S(1)}, bf16[64,2176]{1,0:T(8,128)(2,1)S(1)}, u32[]{:S(2)}, u32[]{:S(2)}) collective-permute-start(bf16[64,2176]{1,0:T(8,128)(2,1)S(1)} %collective-permute-done.5.refs_1_), channel_id=1, source_target_pairs={{0,2},{1,3},{2,0},{3,1},{4,6},{5,7},{6,4},{7,5},{8,10},{9,11},{10,... | collective-permute-start | bytes 835592 | tf_op jit(solution)/shard_map/ppermute | solution.py:242
  35.8 5.9 %collective-permute-start.10 = (bf16[128,2048]{1,0:T(8,128)(2,1)S(1)}, bf16[128,2048]{1,0:T(8,128)(2,1)S(1)}, u32[]{:S(2)}, u32[]{:S(2)}) collective-permute-start(bf16[128,2048]{1,0:T(8,128)(2,1)S(1)} %get-tuple-element.33), channel_id=1, source_target_pairs={{0,1},{1,0},{2,3},{3,2},{4,5},{5,4},{6,7},{7,6},{8,9},{9,8},{10,11... | collective-permute-start | bytes 1572872 | tf_op jit(solution)/shard_map/ppermute | solution.py:242
  36.3 6.2 %collective-permute-start.12 = (bf16[64,2176]{1,0:T(8,128)(2,1)S(1)}, bf16[64,2176]{1,0:T(8,128)(2,1)S(1)}, u32[]{:S(2)}, u32[]{:S(2)}) collective-permute-start(bf16[64,2176]{1,0:T(8,128)(2,1)S(1)} %collective-permute-done.5.refs_1_), channel_id=1, source_target_pairs={{0,1},{1,0},{2,3},{3,2},{4,5},{5,4},{6,7},{7,6},{8,9},{9,8},{10,11... | collective-permute-start | bytes 835592 | tf_op jit(solution)/shard_map/ppermute | solution.py:242
  39.1 6.9 %collective-permute-start.20 = (bf16[128,2048]{1,0:T(8,128)(2,1)S(1)}, bf16[128,2048]{1,0:T(8,128)(2,1)S(1)}, u32[]{:S(2)}, u32[]{:S(2)}) collective-permute-start(bf16[128,2048]{1,0:T(8,128)(2,1)S(1)} %get-tuple-element.40), channel_id=1, source_target_pairs={{0,1},{1,0},{2,3},{3,2},{4,5},{5,4},{6,7},{7,6},{8,9},{9,8},{10,11... | collective-permute-start | bytes 1572872 | tf_op jit(solution)/shard_map/ppermute | solution.py:242
  41.5 1.6 %collective-permute-start.13 = (bf16[64,2176]{1,0:T(8,128)(2,1)S(1)}, bf16[64,2176]{1,0:T(8,128)(2,1)S(1)}, u32[]{:S(2)}, u32[]{:S(2)}) collective-permute-start(bf16[64,2176]{1,0:T(8,128)(2,1)S(1)} %collective-permute-done.11.refs_2_), channel_id=1, source_target_pairs={{0,1},{1,0},{2,3},{3,2},{4,5},{5,4},{6,7},{7,6},{8,9},{9,8},{10,11... | collective-permute-start | bytes 835592 | tf_op jit(solution)/shard_map/ppermute | solution.py:242
  41.9 8.8 %collective-permute-start.21 = (bf16[64,2048]{1,0:T(8,128)(2,1)S(1)}, bf16[64,2048]{1,0:T(8,128)(2,1)S(1)}, u32[]{:S(2)}, u32[]{:S(2)}) collective-permute-start(bf16[64,2048]{1,0:T(8,128)(2,1)S(1)} %fusion.8), channel_id=1, source_target_pairs={{0,2},{1,3},{2,0},{3,1},{4,6},{5,7},{6,4},{7,5},{8,10},{9,11},{10,... | collective-permute-start | bytes 786440 | tf_op jit(solution)/shard_map/ppermute | solution.py:242
  45.8 8.9 %collective-permute-start.14 = (bf16[128,2048]{1,0:T(8,128)(2,1)S(1)}, bf16[128,2048]{1,0:T(8,128)(2,1)S(1)}, u32[]{:S(2)}, u32[]{:S(2)}) collective-permute-start(bf16[128,2048]{1,0:T(8,128)(2,1)S(1)} %get-tuple-element.36), channel_id=1, source_target_pairs={{0,1},{1,0},{2,3},{3,2},{4,5},{5,4},{6,7},{7,6},{8,9},{9,8},{10,11... | collective-permute-start | bytes 1572872 | tf_op jit(solution)/shard_map/ppermute | solution.py:242
  50.8 17.9 %collective-permute-start.24 = (bf16[64,2048]{1,0:T(8,128)(2,1)S(1)}, bf16[64,2048]{1,0:T(8,128)(2,1)S(1)}, u32[]{:S(2)}, u32[]{:S(2)}) collective-permute-start(bf16[64,2048]{1,0:T(8,128)(2,1)S(1)} %fusion.3), channel_id=1, source_target_pairs={{0,8},{1,9},{2,10},{3,11},{4,12},{5,13},{6,14},{7,15},{8,0},{9,1},... | collective-permute-start | bytes 786440 | tf_op jit(solution)/shard_map/ppermute | solution.py:242
  54.1 9.2 %collective-permute-start.22 = (bf16[64,2048]{1,0:T(8,128)(2,1)S(1)}, bf16[64,2048]{1,0:T(8,128)(2,1)S(1)}, u32[]{:S(2)}, u32[]{:S(2)}) collective-permute-start(bf16[64,2048]{1,0:T(8,128)(2,1)S(1)} %fusion.4), channel_id=1, source_target_pairs={{0,2},{1,3},{2,0},{3,1},{4,6},{5,7},{6,4},{7,5},{8,10},{9,11},{10,... | collective-permute-start | bytes 786440 | tf_op jit(solution)/shard_map/ppermute | solution.py:242
  54.8 12.6 %collective-permute-start.15 = (bf16[64,2048]{1,0:T(8,128)(2,1)S(1)}, bf16[64,2048]{1,0:T(8,128)(2,1)S(1)}, u32[]{:S(2)}, u32[]{:S(2)}) collective-permute-start(bf16[64,2048]{1,0:T(8,128)(2,1)S(1)} %fusion.7), channel_id=1, source_target_pairs={{0,2},{1,3},{2,0},{3,1},{4,6},{5,7},{6,4},{7,5},{8,10},{9,11},{10,... | collective-permute-start | bytes 786440 | tf_op jit(solution)/shard_map/ppermute | solution.py:242
  63.4 12.1 %collective-permute-start.23 = (bf16[64,2048]{1,0:T(8,128)(2,1)S(1)}, bf16[64,2048]{1,0:T(8,128)(2,1)S(1)}, u32[]{:S(2)}, u32[]{:S(2)}) collective-permute-start(bf16[64,2048]{1,0:T(8,128)(2,1)S(1)} %fusion.6), channel_id=1, source_target_pairs={{0,4},{1,5},{2,6},{3,7},{4,0},{5,1},{6,2},{7,3},{8,12},{9,13},{10,... | collective-permute-start | bytes 786440 | tf_op jit(solution)/shard_map/ppermute | solution.py:242
  67.5 12.1 %collective-permute-start.25 = (bf16[64,2048]{1,0:T(8,128)(2,1)S(1)}, bf16[64,2048]{1,0:T(8,128)(2,1)S(1)}, u32[]{:S(2)}, u32[]{:S(2)}) collective-permute-start(bf16[64,2048]{1,0:T(8,128)(2,1)S(1)} %fusion.1), channel_id=1, source_target_pairs={{0,12},{1,13},{2,14},{3,15},{4,8},{5,9},{6,10},{7,11},{8,4},{9,5},... | collective-permute-start | bytes 786440 | tf_op jit(solution)/shard_map/ppermute | solution.py:242
  67.5 12.0 %collective-permute-start.16 = (bf16[64,2048]{1,0:T(8,128)(2,1)S(1)}, bf16[64,2048]{1,0:T(8,128)(2,1)S(1)}, u32[]{:S(2)}, u32[]{:S(2)}) collective-permute-start(bf16[64,2048]{1,0:T(8,128)(2,1)S(1)} %fusion.9), channel_id=1, source_target_pairs={{0,2},{1,3},{2,0},{3,1},{4,6},{5,7},{6,4},{7,5},{8,10},{9,11},{10,... | collective-permute-start | bytes 786440 | tf_op jit(solution)/shard_map/ppermute | solution.py:242

commit v4 on v3

--- a/solution.py
+++ b/solution.py
@@ -10,6 +10,7 @@
 LANES = 128
 CHUNK = 256
 FIRST = 'K0'
+KERNEL_FLOPS = 1
 FIRST_LIMIT = 41 * 2**20
 STEPS = [
     ('A4', []),
@@ -21,20 +22,20 @@
     ('A6', []),
     ('A5', []),
     ('A7', []),
-    ('A10', []),
+    ('A10', ['A5']),
     ('A9', []),
     ('A11', []),
     ('A14', []),
     ('A13', []),
     ('A15', []),
     ('K0', []),
-    ('K8', ['K0']),
+    ('K8', []),
     ('O8', []),
     ('X8', []),
-    ('K4', ['K0']),
+    ('K4', []),
     ('O0', []),
     ('O4', []),
-    ('X4', ['X8']),
+    ('X4', []),
     ('K12', ['O8']),
     ('O12', []),
     ('X12', []),
@@ -231,7 +232,7 @@
         scratch_shapes=[pltpu.VMEM((rows, hidden_width), jnp.bfloat16)]
         + [pltpu.SemaphoreType.DMA((6,))] * first,
         compiler_params=pltpu.CompilerParams(vmem_limit_bytes=FIRST_LIMIT if first else VMEM_LIMIT),
-        cost_estimate=pl.CostEstimate(flops=1, bytes_accessed=1, transcendentals=0),
+        cost_estimate=pl.CostEstimate(flops=KERNEL_FLOPS, bytes_accessed=1, transcendentals=0),
     )(me, *blocks, *weights)
 
 
@@ -257,7 +258,7 @@
             weights = tuple(array * one for array in weights)
             done[step] = weights[-1]
         elif kind == "A":
-            bit = number & -number if number % 4 else 1 << (number.bit_length() - 1)
+            bit = number & -number
             done[step] = exchange(after(done["A%d" % (number - bit)], ties), bit)
         elif kind == "B":
             pair = jnp.concatenate([done["A%d" % number], done["A%d" % (number + 2)]], axis=0)
@@ -272,7 +273,7 @@
             done[step] = parts[0]
             own[number], other[number] = parts[:2], parts[2]
         elif kind == "O":
-            got = exchange(other[number], 1).astype(jnp.float32)
+            got = exchange(after(other[number], ties), 1).astype(jnp.float32)
             count = got.shape[0] // 2
             done[step] = (own[number][1] + got[count:]).astype(jnp.bfloat16)
             own[number] = own[number][0] + got[:count]
@@ -280,10 +281,9 @@
             done[step] = exchange(after(done["O%d" % number], ties), 2)
             sums[number] = own[number] + done[step].astype(jnp.float32)
         elif kind == "Z":
-            done[step] = exchange(after(sums[number].astype(jnp.bfloat16), ties), number)
-    combined = sums[0]
-    for z in range(4, peer_count, 4):
-        combined = combined + done["Z%d" % z].astype(jnp.float32)
+            total = sums[number] + done["Z8"].astype(jnp.float32) if number == 12 else sums[number]
+            done[step] = exchange(after(total.astype(jnp.bfloat16), ties), 12 if number == 12 else 4)
+    combined = sums[0] + done["Z4"].astype(jnp.float32) + done["Z12"].astype(jnp.float32)
     return combined.astype(jnp.bfloat16)
 
 
@@ -291,8 +291,7 @@
     peer_count = lax.axis_size("expert")
     local_experts = w_gate.shape[0]
     capacity = 2 * tokens.shape[0] * expert_ids.shape[1] // (peer_count * local_experts)
-    power_of_two = peer_count & (peer_count - 1) == 0
-    whole = capacity >= tokens.shape[0] and local_experts == 1 and peer_count >= 4 and power_of_two
+    whole = capacity >= tokens.shape[0] and local_experts == 1 and peer_count == 16
     layer = gathered if whole else routed
     return layer(tokens, scales, expert_ids, gate_weights, w_gate, w_up, w_down)
 

time: 80.6 us -> 73.9 us (0.917)
  waiting for transfers between devices: 41.5 us -> 26.8 us
  starting transfers between devices: 19.6 us -> 26.8 us
    ppermute x26, waiting for transfers between devices: 41.5 us -> 26.8 us  [exchange(): lax.ppermute(array, 'expert', [(i, i ^ mask) for i in range(peer_count)])]
    ppermute x26, starting transfers between devices: 19.6 us -> 26.8 us  [exchange(): lax.ppermute(array, 'expert', [(i, i ^ mask) for i in range(peer_count)])]
  transfers between devices with their start and end apart: 26 -> 26, of which waited for: 12 -> 9; matrix products, arithmetic and copies ran while one was open for 1% -> 1% of each run, Pallas kernels for 18% -> 20%
where the time goes in v4:
time: 73.9 us; the launch traced here: 73 us
  starting transfers between devices  26.8 us (36%)
  waiting for transfers between devices  26.8 us (36%)
  Pallas kernels  16.4 us (22%)
  other arithmetic  1.78 us (2%)
  local copies, waits for them, and re-layouts  0.95 us (1%)
    ppermute x26, waiting for transfers between devices, exchange(): lax.ppermute(array, 'expert', [(i, i ^ mask) for i in range(peer_count)])  26.8 us
    ppermute x26, starting transfers between devices, exchange(): lax.ppermute(array, 'expert', [(i, i ^ mask) for i in range(peer_count)])  26.8 us
    pallas_call x4, Pallas kernels, weighted_outputs(): pl.pallas_call(functools.partial(first_kernel if first else expert_kernel...  14.5 us
    pallas_call x1, Pallas kernels, pack_rows(): pl.pallas_call(functools.partial(pack_kernel, expert_total), in_specs=[pl...  1.94 us
  transfers between devices with their start and end apart: 26, of which 9 were waited for; matrix products, arithmetic and copies ran while one was open for 1% of the time, Pallas kernels for 20%

profile of v4, /device:TPU:12, one launch (start us, length us, event | category | flops | bytes accessed | tf_op | source)
XLA Modules:
  0.0 73.0 jit_solution(5002875264591810690)
XLA Ops:
  0.0 1.9 %shard_map.73.refs_1_ = bf16[64,2176]{1,0:T(8,128)(2,1)} custom-call(bf16[64,2048]{1,0:T(8,128)(2,1)} %refs_0_.1, bf16[16,64]{1,0:T(8,128)(2,1)} %bitcast.4, s32[8,64]{1,0:T(8,128)} %bitcast.5, f32[8,64]{1,0:T(8,128)} %bitcast.6), custom_call_target="tpu_custom_call" | custom-call | flops 1 | bytes 1 | tf_op jit(solution)/shard_map/pallas_call | solution.py:155
  1.9 0.5 collective-permute-start.6
  2.5 1.5 %collective-permute-start = (bf16[64,2176]{1,0:T(8,128)(2,1)}, bf16[64,2176]{1,0:T(8,128)(2,1)S(1)}, u32[]{:S(2)}, u32[]{:S(2)}) collective-permute-start(bf16[64,2176]{1,0:T(8,128)(2,1)} %shard_map.73.refs_1_), channel_id=1, source_target_pairs={{0,2},{1,3},{2,0},{3,1},{4,6},{5,7},{6,4},{7,5},{8,10},{9,11},{10,... | collective-permute-start | bytes 835592 | tf_op jit(solution)/shard_map/ppermute | solution.py:243
  4.0 2.6 %collective-permute-start.4 = (bf16[64,2176]{1,0:T(8,128)(2,1)}, bf16[64,2176]{1,0:T(8,128)(2,1)S(1)}, u32[]{:S(2)}, u32[]{:S(2)}) collective-permute-start(bf16[64,2176]{1,0:T(8,128)(2,1)} %shard_map.73.refs_1_), channel_id=1, source_target_pairs={{0,8},{1,9},{2,10},{3,11},{4,12},{5,13},{6,14},{7,15},{8,0},{9,1},... | collective-permute-start | bytes 835592 | tf_op jit(solution)/shard_map/ppermute | solution.py:243
  6.5 6.8 %collective-permute-done.6.refs_1_ = bf16[64,2176]{1,0:T(8,128)(2,1)S(1)} collective-permute-done((bf16[64,2176]{1,0:T(8,128)(2,1)}, bf16[64,2176]{1,0:T(8,128)(2,1)S(1)}, u32[]{:S(2)}, u32[]{:S(2)}) %collective-permute-start.6) | collective-permute-done | bytes 278560 | tf_op jit(solution)/shard_map/ppermute | solution.py:243
  13.3 0.5 collective-permute-start.1
  13.8 2.4 %collective-permute-start.18 = (bf16[64,2176]{1,0:T(8,128)(2,1)S(1)}, bf16[64,2176]{1,0:T(8,128)(2,1)S(1)}, u32[]{:S(2)}, u32[]{:S(2)}) collective-permute-start(bf16[64,2176]{1,0:T(8,128)(2,1)S(1)} %collective-permute-done.6.refs_1_), channel_id=1, source_target_pairs={{0,2},{1,3},{2,0},{3,1},{4,6},{5,7},{6,4},{7,5},{8,10},{9,11},{10,... | collective-permute-start | bytes 835592 | tf_op jit(solution)/shard_map/ppermute | solution.py:243
  16.3 1.9 %collective-permute-done.4.refs_1_ = bf16[64,2176]{1,0:T(8,128)(2,1)S(1)} collective-permute-done((bf16[64,2176]{1,0:T(8,128)(2,1)}, bf16[64,2176]{1,0:T(8,128)(2,1)S(1)}, u32[]{:S(2)}, u32[]{:S(2)}) %collective-permute-start.4) | collective-permute-done | bytes 278560 | tf_op jit(solution)/shard_map/ppermute | solution.py:243
  18.2 1.0 %collective-permute-start.8 = (bf16[64,2176]{1,0:T(8,128)(2,1)S(1)}, bf16[64,2176]{1,0:T(8,128)(2,1)S(1)}, u32[]{:S(2)}, u32[]{:S(2)}) collective-permute-start(bf16[64,2176]{1,0:T(8,128)(2,1)S(1)} %collective-permute-done.4.refs_1_), channel_id=1, source_target_pairs={{0,2},{1,3},{2,0},{3,1},{4,6},{5,7},{6,4},{7,5},{8,10},{9,11},{10,... | collective-permute-start | bytes 835592 | tf_op jit(solution)/shard_map/ppermute | solution.py:243
  19.2 1.9 %collective-permute-start.5 = (bf16[64,2176]{1,0:T(8,128)(2,1)S(1)}, bf16[64,2176]{1,0:T(8,128)(2,1)S(1)}, u32[]{:S(2)}, u32[]{:S(2)}) collective-permute-start(bf16[64,2176]{1,0:T(8,128)(2,1)S(1)} %collective-permute-done.4.refs_1_), channel_id=1, source_target_pairs={{0,4},{1,5},{2,6},{3,7},{4,0},{5,1},{6,2},{7,3},{8,12},{9,13},{10,... | collective-permute-start | bytes 835592 | tf_op jit(solution)/shard_map/ppermute | solution.py:243
  21.1 1.0 %copy-done = bf16[64,2176]{1,0:T(8,128)(2,1)S(1)} copy-done((bf16[64,2176]{1,0:T(8,128)(2,1)S(1)}, bf16[64,2176]{1,0:T(8,128)(2,1)}, u32[]{:S(2)}) %copy-start) | copy-done | bytes 278552
  22.0 6.5 %shard_map.74 = (f32[64,2048]{1,0:T(8,128)S(1)}, f32[64,2048]{1,0:T(8,128)S(1)}, bf16[128,2048]{1,0:T(8,128)(2,1)S(1)}, bf16[1,2048,768]{2,1,0:T(8,128)(2,1)S(1)...) custom-call(s32[1]{0:T(128)} %bitcast.refs_0_, bf16[64,2176]{1,0:T(8,128)(2,1)S(1)} %copy-done, ...), custom_call_target="tpu_custom_call" | custom-call | flops 1 | bytes 1 | tf_op jit(solution)/shard_map/pallas_call | solution.py:220
  28.6 0.5 collective-permute-start.19
  29.2 0.4 collective-permute-done.8.refs_2_
  29.6 1.7 %collective-permute-start.12 = (bf16[64,2176]{1,0:T(8,128)(2,1)S(1)}, bf16[64,2176]{1,0:T(8,128)(2,1)S(1)}, u32[]{:S(2)}, u32[]{:S(2)}) collective-permute-start(bf16[64,2176]{1,0:T(8,128)(2,1)S(1)} %collective-permute-done.5.refs_1_), channel_id=1, source_target_pairs={{0,2},{1,3},{2,0},{3,1},{4,6},{5,7},{6,4},{7,5},{8,10},{9,11},{10,... | collective-permute-start | bytes 835592 | tf_op jit(solution)/shard_map/ppermute | solution.py:243
  31.3 2.7 %shard_map.77 = (f32[64,2048]{1,0:T(8,128)S(1)}, f32[64,2048]{1,0:T(8,128)S(1)}, bf16[128,2048]{1,0:T(8,128)(2,1)S(1)}) custom-call(s32[1]{0:T(128)} %bitcast.refs_0_, bf16[64,2176]{1,0:T(8,128)(2,1)S(1)} %collective-permute-done.6.refs_1_, bf16[64,2176]{1,0:T(8,128)(2,1)S(1)} %collective-permute-done.18.refs_2_, ...), custom_call_target="tpu_custom_call" | custom-call | flops 1 | bytes 1 | tf_op jit(solution)/shard_map/pallas_call | solution.py:220
  34.3 2.7 %shard_map.75 = (f32[64,2048]{1,0:T(8,128)S(1)}, f32[64,2048]{1,0:T(8,128)S(1)}, bf16[128,2048]{1,0:T(8,128)(2,1)S(1)}) custom-call(s32[1]{0:T(128)} %bitcast.refs_0_, bf16[64,2176]{1,0:T(8,128)(2,1)S(1)} %collective-permute-done.4.refs_1_, bf16[64,2176]{1,0:T(8,128)(2,1)S(1)} %collective-permute-done.8.refs_2_, ...), custom_call_target="tpu_custom_call" | custom-call | flops 1 | bytes 1 | tf_op jit(solution)/shard_map/pallas_call | solution.py:220
  37.0 0.4 collective-permute-start.11
  37.6 1.1 %collective-permute-done.12.refs_2_ = bf16[64,2176]{1,0:T(8,128)(2,1)S(1)} collective-permute-done((bf16[64,2176]{1,0:T(8,128)(2,1)S(1)}, bf16[64,2176]{1,0:T(8,128)(2,1)S(1)}, u32[]{:S(2)}, u32[]{:S(2)}) %collective-permute-start.12) | collective-permute-done | bytes 278560 | tf_op jit(solution)/shard_map/ppermute | solution.py:243
  39.1 1.8 %collective-permute-start.23 = (bf16[64,2048]{1,0:T(8,128)(2,1)S(1)}, bf16[64,2048]{1,0:T(8,128)(2,1)S(1)}, u32[]{:S(2)}, u32[]{:S(2)}) collective-permute-start(bf16[64,2048]{1,0:T(8,128)(2,1)S(1)} %fusion.9), channel_id=1, source_target_pairs={{0,2},{1,3},{2,0},{3,1},{4,6},{5,7},{6,4},{7,5},{8,10},{9,11},{10,... | collective-permute-start | bytes 786440 | tf_op jit(solution)/shard_map/ppermute | solution.py:243
  40.9 2.7 %shard_map.76 = (f32[64,2048]{1,0:T(8,128)S(1)}, f32[64,2048]{1,0:T(8,128)S(1)}, bf16[128,2048]{1,0:T(8,128)(2,1)S(1)}) custom-call(s32[1]{0:T(128)} %bitcast.refs_0_, bf16[64,2176]{1,0:T(8,128)(2,1)S(1)} %collective-permute-done.5.refs_1_, bf16[64,2176]{1,0:T(8,128)(2,1)S(1)} %collective-permute-done.12.refs_2_, ...), custom_call_target="tpu_custom_call" | custom-call | flops 1 | bytes 1 | tf_op jit(solution)/shard_map/pallas_call | solution.py:220
  44.0 1.0 %collective-permute-start.21 = (bf16[64,2048]{1,0:T(8,128)(2,1)S(1)}, bf16[64,2048]{1,0:T(8,128)(2,1)S(1)}, u32[]{:S(2)}, u32[]{:S(2)}) collective-permute-start(bf16[64,2048]{1,0:T(8,128)(2,1)S(1)} %fusion.5), channel_id=1, source_target_pairs={{0,2},{1,3},{2,0},{3,1},{4,6},{5,7},{6,4},{7,5},{8,10},{9,11},{10,... | collective-permute-start | bytes 786440 | tf_op jit(solution)/shard_map/ppermute | solution.py:243
  45.0 3.3 %collective-permute-done.23 = bf16[64,2048]{1,0:T(8,128)(2,1)S(1)} collective-permute-done((bf16[64,2048]{1,0:T(8,128)(2,1)S(1)}, bf16[64,2048]{1,0:T(8,128)(2,1)S(1)}, u32[]{:S(2)}, u32[]{:S(2)}) %collective-permute-start.23) | collective-permute-done | bytes 262176 | tf_op jit(solution)/shard_map/ppermute | solution.py:243
  48.4 2.4 %collective-permute-start.24 = (bf16[64,2048]{1,0:T(8,128)(2,1)S(1)}, bf16[64,2048]{1,0:T(8,128)(2,1)S(1)}, u32[]{:S(2)}, u32[]{:S(2)}) collective-permute-start(bf16[64,2048]{1,0:T(8,128)(2,1)S(1)} %fusion.1), channel_id=1, source_target_pairs={{0,4},{1,5},{2,6},{3,7},{4,0},{5,1},{6,2},{7,3},{8,12},{9,13},{10,... | collective-permute-start | bytes 786440 | tf_op jit(solution)/shard_map/ppermute | solution.py:243
  51.0 1.8 %collective-permute-start.16 = (bf16[64,2048]{1,0:T(8,128)(2,1)S(1)}, bf16[64,2048]{1,0:T(8,128)(2,1)S(1)}, u32[]{:S(2)}, u32[]{:S(2)}) collective-permute-start(bf16[64,2048]{1,0:T(8,128)(2,1)S(1)} %fusion.8), channel_id=1, source_target_pairs={{0,2},{1,3},{2,0},{3,1},{4,6},{5,7},{6,4},{7,5},{8,10},{9,11},{10,... | collective-permute-start | bytes 786440 | tf_op jit(solution)/shard_map/ppermute | solution.py:243
  52.8 1.1 %collective-permute-done.21 = bf16[64,2048]{1,0:T(8,128)(2,1)S(1)} collective-permute-done((bf16[64,2048]{1,0:T(8,128)(2,1)S(1)}, bf16[64,2048]{1,0:T(8,128)(2,1)S(1)}, u32[]{:S(2)}, u32[]{:S(2)}) %collective-permute-start.21) | collective-permute-done | bytes 262176 | tf_op jit(solution)/shard_map/ppermute | solution.py:243
  54.0 2.4 %collective-permute-start.22 = (bf16[64,2048]{1,0:T(8,128)(2,1)S(1)}, bf16[64,2048]{1,0:T(8,128)(2,1)S(1)}, u32[]{:S(2)}, u32[]{:S(2)}) collective-permute-start(bf16[64,2048]{1,0:T(8,128)(2,1)S(1)} %fusion.7), channel_id=1, source_target_pairs={{0,4},{1,5},{2,6},{3,7},{4,0},{5,1},{6,2},{7,3},{8,12},{9,13},{10,... | collective-permute-start | bytes 786440 | tf_op jit(solution)/shard_map/ppermute | solution.py:243
  56.6 2.5 %collective-permute-done.16 = bf16[64,2048]{1,0:T(8,128)(2,1)S(1)} collective-permute-done((bf16[64,2048]{1,0:T(8,128)(2,1)S(1)}, bf16[64,2048]{1,0:T(8,128)(2,1)S(1)}, u32[]{:S(2)}, u32[]{:S(2)}) %collective-permute-start.16) | collective-permute-done | bytes 262176 | tf_op jit(solution)/shard_map/ppermute | solution.py:243
  59.3 1.7 %collective-permute-start.25 = (bf16[64,2048]{1,0:T(8,128)(2,1)S(1)}, bf16[64,2048]{1,0:T(8,128)(2,1)S(1)}, u32[]{:S(2)}, u32[]{:S(2)}) collective-permute-start(bf16[64,2048]{1,0:T(8,128)(2,1)S(1)} %fusion.4), channel_id=1, source_target_pairs={{0,12},{1,13},{2,14},{3,15},{4,8},{5,9},{6,10},{7,11},{8,4},{9,5},... | collective-permute-start | bytes 786440 | tf_op jit(solution)/shard_map/ppermute | solution.py:243
  60.9 1.7 %collective-permute-start.17 = (bf16[64,2048]{1,0:T(8,128)(2,1)S(1)}, bf16[64,2048]{1,0:T(8,128)(2,1)S(1)}, u32[]{:S(2)}, u32[]{:S(2)}) collective-permute-start(bf16[64,2048]{1,0:T(8,128)(2,1)S(1)} %fusion.10), channel_id=1, source_target_pairs={{0,2},{1,3},{2,0},{3,1},{4,6},{5,7},{6,4},{7,5},{8,10},{9,11},{10,... | collective-permute-start | bytes 786440 | tf_op jit(solution)/shard_map/ppermute | solution.py:243
  62.7 9.4 %collective-permute-done.25 = bf16[64,2048]{1,0:T(8,128)(2,1)S(1)} collective-permute-done((bf16[64,2048]{1,0:T(8,128)(2,1)S(1)}, bf16[64,2048]{1,0:T(8,128)(2,1)S(1)}, u32[]{:S(2)}, u32[]{:S(2)}) %collective-permute-start.25) | collective-permute-done | bytes 262176 | tf_op jit(solution)/shard_map/ppermute | solution.py:243
  72.1 0.9 %fusion.14 = bf16[64,2048]{1,0:T(8,128)(2,1)} fusion(f32[64,2048]{1,0:T(8,128)S(1)} %get-tuple-element.23, f32[128,2048]{1,0:T(8,128)S(1)} %convert_element_type.57, bf16[64,2048]{1,0:T(8,128)(2,1)S(1)} %collective-permute-done.25, bf16[64,2048]{1,0:T(8,128)(2,1)S(1)} %collective-permute-done.22, bf16[64,2048]{1,0:T(8,128)(2,1)S(1)} %collective-permute-done.17), kind=kLoop, calls=%fused_computation.22 | loop fusion | flops 1048576 | bytes 2097152 | tf_op jit(solution)/shard_map/convert_element_type | solution.py:287
  (39 shorter events, 2.1 us)
Async XLA Ops:
  1.9 11.4 %collective-permute-start.6 = (bf16[64,2176]{1,0:T(8,128)(2,1)}, bf16[64,2176]{1,0:T(8,128)(2,1)S(1)}, u32[]{:S(2)}, u32[]{:S(2)}) collective-permute-start(bf16[64,2176]{1,0:T(8,128)(2,1)} %shard_map.73.refs_1_), channel_id=1, source_target_pairs={{0,4},{1,5},{2,6},{3,7},{4,0},{5,1},{6,2},{7,3},{8,12},{9,13},{10,... | collective-permute-start | bytes 835592 | tf_op jit(solution)/shard_map/ppermute | solution.py:243
  2.5 11.4 %collective-permute-start = (bf16[64,2176]{1,0:T(8,128)(2,1)}, bf16[64,2176]{1,0:T(8,128)(2,1)S(1)}, u32[]{:S(2)}, u32[]{:S(2)}) collective-permute-start(bf16[64,2176]{1,0:T(8,128)(2,1)} %shard_map.73.refs_1_), channel_id=1, source_target_pairs={{0,2},{1,3},{2,0},{3,1},{4,6},{5,7},{6,4},{7,5},{8,10},{9,11},{10,... | collective-permute-start | bytes 835592 | tf_op jit(solution)/shard_map/ppermute | solution.py:243
  4.0 14.3 %collective-permute-start.4 = (bf16[64,2176]{1,0:T(8,128)(2,1)}, bf16[64,2176]{1,0:T(8,128)(2,1)S(1)}, u32[]{:S(2)}, u32[]{:S(2)}) collective-permute-start(bf16[64,2176]{1,0:T(8,128)(2,1)} %shard_map.73.refs_1_), channel_id=1, source_target_pairs={{0,8},{1,9},{2,10},{3,11},{4,12},{5,13},{6,14},{7,15},{8,0},{9,1},... | collective-permute-start | bytes 835592 | tf_op jit(solution)/shard_map/ppermute | solution.py:243
  13.3 4.9 %collective-permute-start.7 = (bf16[64,2176]{1,0:T(8,128)(2,1)S(1)}, bf16[64,2176]{1,0:T(8,128)(2,1)S(1)}, u32[]{:S(2)}, u32[]{:S(2)}) collective-permute-start(bf16[64,2176]{1,0:T(8,128)(2,1)S(1)} %collective-permute-done.6.refs_1_), channel_id=1, source_target_pairs={{0,1},{1,0},{2,3},{3,2},{4,5},{5,4},{6,7},{7,6},{8,9},{9,8},{10,11... | collective-permute-start | bytes 835592 | tf_op jit(solution)/shard_map/ppermute | solution.py:243
  13.3 7.7 %collective-permute-start.1 = (bf16[64,2176]{1,0:T(8,128)(2,1)}, bf16[64,2176]{1,0:T(8,128)(2,1)S(1)}, u32[]{:S(2)}, u32[]{:S(2)}) collective-permute-start(bf16[64,2176]{1,0:T(8,128)(2,1)} %shard_map.73.refs_1_), channel_id=1, source_target_pairs={{0,1},{1,0},{2,3},{3,2},{4,5},{5,4},{6,7},{7,6},{8,9},{9,8},{10,11... | collective-permute-start | bytes 835592 | tf_op jit(solution)/shard_map/ppermute | solution.py:243
  13.8 7.2 %collective-permute-start.2 = (bf16[64,2176]{1,0:T(8,128)(2,1)S(1)}, bf16[64,2176]{1,0:T(8,128)(2,1)S(1)}, u32[]{:S(2)}, u32[]{:S(2)}) collective-permute-start(bf16[64,2176]{1,0:T(8,128)(2,1)S(1)} %collective-permute-done.refs_2_), channel_id=1, source_target_pairs={{0,1},{1,0},{2,3},{3,2},{4,5},{5,4},{6,7},{7,6},{8,9},{9,8},{10,11... | collective-permute-start | bytes 835592 | tf_op jit(solution)/shard_map/ppermute | solution.py:243
  13.8 14.7 %collective-permute-start.18 = (bf16[64,2176]{1,0:T(8,128)(2,1)S(1)}, bf16[64,2176]{1,0:T(8,128)(2,1)S(1)}, u32[]{:S(2)}, u32[]{:S(2)}) collective-permute-start(bf16[64,2176]{1,0:T(8,128)(2,1)S(1)} %collective-permute-done.6.refs_1_), channel_id=1, source_target_pairs={{0,2},{1,3},{2,0},{3,1},{4,6},{5,7},{6,4},{7,5},{8,10},{9,11},{10,... | collective-permute-start | bytes 835592 | tf_op jit(solution)/shard_map/ppermute | solution.py:243
  18.2 11.3 %collective-permute-start.8 = (bf16[64,2176]{1,0:T(8,128)(2,1)S(1)}, bf16[64,2176]{1,0:T(8,128)(2,1)S(1)}, u32[]{:S(2)}, u32[]{:S(2)}) collective-permute-start(bf16[64,2176]{1,0:T(8,128)(2,1)S(1)} %collective-permute-done.4.refs_1_), channel_id=1, source_target_pairs={{0,2},{1,3},{2,0},{3,1},{4,6},{5,7},{6,4},{7,5},{8,10},{9,11},{10,... | collective-permute-start | bytes 835592 | tf_op jit(solution)/shard_map/ppermute | solution.py:243
  19.2 10.4 %collective-permute-start.5 = (bf16[64,2176]{1,0:T(8,128)(2,1)S(1)}, bf16[64,2176]{1,0:T(8,128)(2,1)S(1)}, u32[]{:S(2)}, u32[]{:S(2)}) collective-permute-start(bf16[64,2176]{1,0:T(8,128)(2,1)S(1)} %collective-permute-done.4.refs_1_), channel_id=1, source_target_pairs={{0,4},{1,5},{2,6},{3,7},{4,0},{5,1},{6,2},{7,3},{8,12},{9,13},{10,... | collective-permute-start | bytes 835592 | tf_op jit(solution)/shard_map/ppermute | solution.py:243
  21.1 1.0 %copy-start = (bf16[64,2176]{1,0:T(8,128)(2,1)S(1)}, bf16[64,2176]{1,0:T(8,128)(2,1)}, u32[]{:S(2)}) copy-start(bf16[64,2176]{1,0:T(8,128)(2,1)} %shard_map.73.refs_1_) | copy-start | bytes 835588
  28.5 10.2 %collective-permute-start.3 = (bf16[128,2048]{1,0:T(8,128)(2,1)S(1)}, bf16[128,2048]{1,0:T(8,128)(2,1)S(1)}, u32[]{:S(2)}, u32[]{:S(2)}) collective-permute-start(bf16[128,2048]{1,0:T(8,128)(2,1)S(1)} %get-tuple-element.24), channel_id=1, source_target_pairs={{0,1},{1,0},{2,3},{3,2},{4,5},{5,4},{6,7},{7,6},{8,9},{9,8},{10,11... | collective-permute-start | bytes 1572872 | tf_op jit(solution)/shard_map/ppermute | solution.py:243
  28.6 2.8 %collective-permute-start.19 = (bf16[64,2176]{1,0:T(8,128)(2,1)S(1)}, bf16[64,2176]{1,0:T(8,128)(2,1)S(1)}, u32[]{:S(2)}, u32[]{:S(2)}) collective-permute-start(bf16[64,2176]{1,0:T(8,128)(2,1)S(1)} %collective-permute-done.18.refs_2_), channel_id=1, source_target_pairs={{0,1},{1,0},{2,3},{3,2},{4,5},{5,4},{6,7},{7,6},{8,9},{9,8},{10,11... | collective-permute-start | bytes 835592 | tf_op jit(solution)/shard_map/ppermute | solution.py:243
  29.1 5.2 %collective-permute-start.9 = (bf16[64,2176]{1,0:T(8,128)(2,1)S(1)}, bf16[64,2176]{1,0:T(8,128)(2,1)S(1)}, u32[]{:S(2)}, u32[]{:S(2)}) collective-permute-start(bf16[64,2176]{1,0:T(8,128)(2,1)S(1)} %collective-permute-done.4.refs_1_), channel_id=1, source_target_pairs={{0,1},{1,0},{2,3},{3,2},{4,5},{5,4},{6,7},{7,6},{8,9},{9,8},{10,11... | collective-permute-start | bytes 835592 | tf_op jit(solution)/shard_map/ppermute | solution.py:243
  29.6 4.7 %collective-permute-start.10 = (bf16[64,2176]{1,0:T(8,128)(2,1)S(1)}, bf16[64,2176]{1,0:T(8,128)(2,1)S(1)}, u32[]{:S(2)}, u32[]{:S(2)}) collective-permute-start(bf16[64,2176]{1,0:T(8,128)(2,1)S(1)} %collective-permute-done.8.refs_2_), channel_id=1, source_target_pairs={{0,1},{1,0},{2,3},{3,2},{4,5},{5,4},{6,7},{7,6},{8,9},{9,8},{10,11... | collective-permute-start | bytes 835592 | tf_op jit(solution)/shard_map/ppermute | solution.py:243
  29.6 9.1 %collective-permute-start.12 = (bf16[64,2176]{1,0:T(8,128)(2,1)S(1)}, bf16[64,2176]{1,0:T(8,128)(2,1)S(1)}, u32[]{:S(2)}, u32[]{:S(2)}) collective-permute-start(bf16[64,2176]{1,0:T(8,128)(2,1)S(1)} %collective-permute-done.5.refs_1_), channel_id=1, source_target_pairs={{0,2},{1,3},{2,0},{3,1},{4,6},{5,7},{6,4},{7,5},{8,10},{9,11},{10,... | collective-permute-start | bytes 835592 | tf_op jit(solution)/shard_map/ppermute | solution.py:243
  34.0 4.8 %collective-permute-start.20 = (bf16[128,2048]{1,0:T(8,128)(2,1)S(1)}, bf16[128,2048]{1,0:T(8,128)(2,1)S(1)}, u32[]{:S(2)}, u32[]{:S(2)}) collective-permute-start(bf16[128,2048]{1,0:T(8,128)(2,1)S(1)} %get-tuple-element.37), channel_id=1, source_target_pairs={{0,1},{1,0},{2,3},{3,2},{4,5},{5,4},{6,7},{7,6},{8,9},{9,8},{10,11... | collective-permute-start | bytes 1572872 | tf_op jit(solution)/shard_map/ppermute | solution.py:243
  37.0 2.0 %collective-permute-start.11 = (bf16[128,2048]{1,0:T(8,128)(2,1)S(1)}, bf16[128,2048]{1,0:T(8,128)(2,1)S(1)}, u32[]{:S(2)}, u32[]{:S(2)}) collective-permute-start(bf16[128,2048]{1,0:T(8,128)(2,1)S(1)} %get-tuple-element.31), channel_id=1, source_target_pairs={{0,1},{1,0},{2,3},{3,2},{4,5},{5,4},{6,7},{7,6},{8,9},{9,8},{10,11... | collective-permute-start | bytes 1572872 | tf_op jit(solution)/shard_map/ppermute | solution.py:243
  37.4 3.6 %collective-permute-start.13 = (bf16[64,2176]{1,0:T(8,128)(2,1)S(1)}, bf16[64,2176]{1,0:T(8,128)(2,1)S(1)}, u32[]{:S(2)}, u32[]{:S(2)}) collective-permute-start(bf16[64,2176]{1,0:T(8,128)(2,1)S(1)} %collective-permute-done.5.refs_1_), channel_id=1, source_target_pairs={{0,1},{1,0},{2,3},{3,2},{4,5},{5,4},{6,7},{7,6},{8,9},{9,8},{10,11... | collective-permute-start | bytes 835592 | tf_op jit(solution)/shard_map/ppermute | solution.py:243
  38.7 2.3 %collective-permute-start.14 = (bf16[64,2176]{1,0:T(8,128)(2,1)S(1)}, bf16[64,2176]{1,0:T(8,128)(2,1)S(1)}, u32[]{:S(2)}, u32[]{:S(2)}) collective-permute-start(bf16[64,2176]{1,0:T(8,128)(2,1)S(1)} %collective-permute-done.12.refs_2_), channel_id=1, source_target_pairs={{0,1},{1,0},{2,3},{3,2},{4,5},{5,4},{6,7},{7,6},{8,9},{9,8},{10,11... | collective-permute-start | bytes 835592 | tf_op jit(solution)/shard_map/ppermute | solution.py:243
  39.1 9.2 %collective-permute-start.23 = (bf16[64,2048]{1,0:T(8,128)(2,1)S(1)}, bf16[64,2048]{1,0:T(8,128)(2,1)S(1)}, u32[]{:S(2)}, u32[]{:S(2)}) collective-permute-start(bf16[64,2048]{1,0:T(8,128)(2,1)S(1)} %fusion.9), channel_id=1, source_target_pairs={{0,2},{1,3},{2,0},{3,1},{4,6},{5,7},{6,4},{7,5},{8,10},{9,11},{10,... | collective-permute-start | bytes 786440 | tf_op jit(solution)/shard_map/ppermute | solution.py:243
  43.6 7.2 %collective-permute-start.15 = (bf16[128,2048]{1,0:T(8,128)(2,1)S(1)}, bf16[128,2048]{1,0:T(8,128)(2,1)S(1)}, u32[]{:S(2)}, u32[]{:S(2)}) collective-permute-start(bf16[128,2048]{1,0:T(8,128)(2,1)S(1)} %get-tuple-element.34), channel_id=1, source_target_pairs={{0,1},{1,0},{2,3},{3,2},{4,5},{5,4},{6,7},{7,6},{8,9},{9,8},{10,11... | collective-permute-start | bytes 1572872 | tf_op jit(solution)/shard_map/ppermute | solution.py:243
  44.0 9.9 %collective-permute-start.21 = (bf16[64,2048]{1,0:T(8,128)(2,1)S(1)}, bf16[64,2048]{1,0:T(8,128)(2,1)S(1)}, u32[]{:S(2)}, u32[]{:S(2)}) collective-permute-start(bf16[64,2048]{1,0:T(8,128)(2,1)S(1)} %fusion.5), channel_id=1, source_target_pairs={{0,2},{1,3},{2,0},{3,1},{4,6},{5,7},{6,4},{7,5},{8,10},{9,11},{10,... | collective-permute-start | bytes 786440 | tf_op jit(solution)/shard_map/ppermute | solution.py:243
  48.4 8.2 %collective-permute-start.24 = (bf16[64,2048]{1,0:T(8,128)(2,1)S(1)}, bf16[64,2048]{1,0:T(8,128)(2,1)S(1)}, u32[]{:S(2)}, u32[]{:S(2)}) collective-permute-start(bf16[64,2048]{1,0:T(8,128)(2,1)S(1)} %fusion.1), channel_id=1, source_target_pairs={{0,4},{1,5},{2,6},{3,7},{4,0},{5,1},{6,2},{7,3},{8,12},{9,13},{10,... | collective-permute-start | bytes 786440 | tf_op jit(solution)/shard_map/ppermute | solution.py:243
  51.0 8.1 %collective-permute-start.16 = (bf16[64,2048]{1,0:T(8,128)(2,1)S(1)}, bf16[64,2048]{1,0:T(8,128)(2,1)S(1)}, u32[]{:S(2)}, u32[]{:S(2)}) collective-permute-start(bf16[64,2048]{1,0:T(8,128)(2,1)S(1)} %fusion.8), channel_id=1, source_target_pairs={{0,2},{1,3},{2,0},{3,1},{4,6},{5,7},{6,4},{7,5},{8,10},{9,11},{10,... | collective-permute-start | bytes 786440 | tf_op jit(solution)/shard_map/ppermute | solution.py:243
  54.0 8.6 %collective-permute-start.22 = (bf16[64,2048]{1,0:T(8,128)(2,1)S(1)}, bf16[64,2048]{1,0:T(8,128)(2,1)S(1)}, u32[]{:S(2)}, u32[]{:S(2)}) collective-permute-start(bf16[64,2048]{1,0:T(8,128)(2,1)S(1)} %fusion.7), channel_id=1, source_target_pairs={{0,4},{1,5},{2,6},{3,7},{4,0},{5,1},{6,2},{7,3},{8,12},{9,13},{10,... | collective-permute-start | bytes 786440 | tf_op jit(solution)/shard_map/ppermute | solution.py:243
  59.3 12.8 %collective-permute-start.25 = (bf16[64,2048]{1,0:T(8,128)(2,1)S(1)}, bf16[64,2048]{1,0:T(8,128)(2,1)S(1)}, u32[]{:S(2)}, u32[]{:S(2)}) collective-permute-start(bf16[64,2048]{1,0:T(8,128)(2,1)S(1)} %fusion.4), channel_id=1, source_target_pairs={{0,12},{1,13},{2,14},{3,15},{4,8},{5,9},{6,10},{7,11},{8,4},{9,5},... | collective-permute-start | bytes 786440 | tf_op jit(solution)/shard_map/ppermute | solution.py:243
  60.9 11.2 %collective-permute-start.17 = (bf16[64,2048]{1,0:T(8,128)(2,1)S(1)}, bf16[64,2048]{1,0:T(8,128)(2,1)S(1)}, u32[]{:S(2)}, u32[]{:S(2)}) collective-permute-start(bf16[64,2048]{1,0:T(8,128)(2,1)S(1)} %fusion.10), channel_id=1, source_target_pairs={{0,2},{1,3},{2,0},{3,1},{4,6},{5,7},{6,4},{7,5},{8,10},{9,11},{10,... | collective-permute-start | bytes 786440 | tf_op jit(solution)/shard_map/ppermute | solution.py:243
